TPU v7x, 128 devices: a whole 4x4x4 slice. The times are simulated.
128 devices in a mesh: section: 2 (over y_hi), row: 16 (over x, z), col: 4 (over y_lo, core).
Axes of the slice: x: 4, y: 4 (y_hi: 2, y_lo: 2; y = y_hi * 2 + y_lo), z: 4, core: 2. Of those that a mesh axis runs over, the one named last changes fastest.
Arguments:
- layer_input: bfloat16 [2, 16, 577, 1024], P('section', 'row', None, 'col'), may hold values from -6 to 6
- cotangent: bfloat16 [2, 16, 577, 1024], P('section', 'row', None, 'col'), may hold values from -6 to 6
- norm1_gain: bfloat16 [2, 1024], P('section', 'col'), may hold values from 0.5 to 1.5
- norm1_shift: bfloat16 [2, 1024], P('section', 'col'), may hold values from -1.75 to 1.75
- qkv_weight: bfloat16 [2, 1024, 3, 1024], P('section', 'row', None, 'col'), may hold values from -0.1875 to 0.1875
- qv_bias: bfloat16 [2, 2, 1024], P('section', None, 'col'), may hold values from -3 to 3
- out_weight: bfloat16 [2, 1024, 1024], P('section', 'col', 'row'), may hold values from -1 to 1
- out_bias: bfloat16 [2, 1024], P('section', 'col'), may hold values from -1.75 to 1.75
- norm2_gain: bfloat16 [2, 1024], P('section', 'col'), may hold values from 0.5 to 1.5
- norm2_shift: bfloat16 [2, 1024], P('section', 'col'), may hold values from -1.75 to 1.75
- up_weight: bfloat16 [2, 1024, 4096], P('section', 'row', 'col'), may hold values from -1 to 1
- up_bias: bfloat16 [2, 4096], P('section', 'col'), may hold values from -3 to 3
- down_weight: bfloat16 [2, 4096, 1024], P('section', 'col', 'row'), may hold values from -0.09375 to 0.09375
- down_bias: bfloat16 [2, 1024], P('section', 'col'), may hold values from -1.75 to 1.75
Outputs:
- final_output: bfloat16 [2, 16, 577, 1024], P('section', 'row', None, 'col')
- input_grad: bfloat16 [2, 16, 577, 1024], P('section', 'row', None, 'col')
- norm1_gain_grad: float32 [2, 1024], P('section', 'col')
- norm1_shift_grad: float32 [2, 1024], P('section', 'col')
- qkv_weight_grad: float32 [2, 1024, 3, 1024], P('section', 'row', None, 'col')
- qv_bias_grad: float32 [2, 2, 1024], P('section', None, 'col')
- out_weight_grad: float32 [2, 1024, 1024], P('section', 'col', 'row')
- out_bias_grad: float32 [2, 1024], P('section', 'col')
- norm2_gain_grad: float32 [2, 1024], P('section', 'col')
- norm2_shift_grad: float32 [2, 1024], P('section', 'col')
- up_weight_grad: float32 [2, 1024, 4096], P('section', 'row', 'col')
- up_bias_grad: float32 [2, 4096], P('section', 'col')
- down_weight_grad: float32 [2, 4096, 1024], P('section', 'col', 'row')
- down_bias_grad: float32 [2, 1024], P('section', 'col')
All inputs are finite; a program needn't handle non-finite values.
Results may differ from a plain program's by a relative error of at most 0.02.
Values may be sent and summed in bfloat16 or wider, within the bound.
No kernel may reach another device: no remote copies, remote signals or barrier semaphores. Data moves between devices by JAX's collectives and lax.ppermute only.
A program may use at most 192 MiB of HBM per device.

v0:
```python
import jax
import jax.numpy as jnp
from jax import lax
from jax.sharding import PartitionSpec as P

HD = 64


EPS = 1e-06


def partner(value, axis, distance):
    return lax.ppermute(value, axis, [(i, i ^ 1 << distance) for i in range(lax.axis_size(axis))])


def exact_gelu(value):
    return jax.nn.gelu(value, approximate=False)


def norm_forward(resid, gain, shift):
    width = resid.shape[-1] * lax.axis_size("col")
    totals = lax.psum((jnp.sum(resid, -1), jnp.sum(resid * resid, -1)), "col")
    center = totals[0] / width
    scale = lax.rsqrt(totals[1] / width - center * center + EPS)
    normal = (resid - center[..., None]) * scale[..., None]
    features = lax.all_gather(
        (normal * gain + shift).astype(jnp.bfloat16), "col", axis=2, tiled=True
    )
    return (normal, scale, features)


def norm_backward(grad, normal, scale, gain):
    width = grad.shape[-1] * lax.axis_size("col")
    scaled = grad * gain
    totals = lax.psum((jnp.sum(scaled, -1), jnp.sum(scaled * normal, -1)), "col")
    result = scale[..., None] * (
        scaled - (totals[0] / width)[..., None] - normal * (totals[1] / width)[..., None]
    )
    return (result, jnp.sum(grad * normal, (0, 1)), jnp.sum(grad, (0, 1)))


def collect(partial_sum):
    return lax.psum_scatter(
        partial_sum.astype(jnp.bfloat16), "col", scatter_dimension=2, tiled=True
    ).astype(jnp.float32)


def spread_grad(grad):
    return lax.all_gather(grad.astype(jnp.bfloat16), "col", axis=2, tiled=True)


def input_sum(partial_sum):
    return lax.psum_scatter(
        partial_sum.astype(jnp.bfloat16), "col", scatter_dimension=2, tiled=True
    ).astype(jnp.float32)


def token_sum(values):
    return jnp.sum(values.astype(jnp.float32), (0, 1))


def attend_forward(block):
    queries, keys, values = block
    scores = jnp.einsum("qhd,khd->hqk", queries, keys, preferred_element_type=jnp.float32) * 0.125
    peak = jnp.max(scores, -1, keepdims=True)
    logsum = peak + jnp.log(jnp.sum(jnp.exp(scores - peak), -1, keepdims=True))
    probs = jnp.exp(scores - logsum).astype(jnp.bfloat16)
    context = jnp.einsum("hqk,khd->qhd", probs, values, preferred_element_type=jnp.float32)
    return (context.astype(jnp.bfloat16), logsum)


def attend_backward(block):
    queries, keys, values, logsum, grad_context = block
    scores = jnp.einsum("qhd,khd->hqk", queries, keys, preferred_element_type=jnp.float32) * 0.125
    probs = jnp.exp(scores - logsum)
    grad_probs = jnp.einsum(
        "qhd,khd->hqk", grad_context, values, preferred_element_type=jnp.float32
    )
    grad_scores = (probs * (grad_probs - jnp.sum(probs * grad_probs, -1, keepdims=True))).astype(
        jnp.bfloat16
    )
    grad_queries = (
        jnp.einsum("hqk,khd->qhd", grad_scores, keys, preferred_element_type=jnp.float32) * 0.125
    )
    grad_keys = (
        jnp.einsum("hqk,qhd->khd", grad_scores, queries, preferred_element_type=jnp.float32) * 0.125
    )
    grad_values = jnp.einsum(
        "hqk,qhd->khd", probs.astype(jnp.bfloat16), grad_context, preferred_element_type=jnp.float32
    )
    return (grad_queries, grad_keys, grad_values)


def layer_forward(resid, weights, params):
    qkv_full, out_full, up_full, down_full = weights
    norm1_gain, norm1_shift, qv_bias, out_bias, norm2_gain, norm2_shift, up_bias, down_bias = params
    images, length, local_width = resid.shape
    heads_here = local_width // HD
    normal_one, scale_one, features_one = norm_forward(resid, norm1_gain, norm1_shift)
    mixed = jnp.einsum("isd,dtc->istc", features_one, qkv_full, preferred_element_type=jnp.float32)
    queries = (
        (mixed[:, :, 0] + qv_bias[0]).astype(jnp.bfloat16).reshape(images, length, heads_here, HD)
    )
    keys = mixed[:, :, 1].astype(jnp.bfloat16).reshape(images, length, heads_here, HD)
    values = (
        (mixed[:, :, 2] + qv_bias[1]).astype(jnp.bfloat16).reshape(images, length, heads_here, HD)
    )
    context, logsum = lax.map(attend_forward, (queries, keys, values))
    context = context.reshape(images, length, local_width)
    attention = (
        collect(jnp.einsum("isc,cd->isd", context, out_full, preferred_element_type=jnp.float32))
        + out_bias
    )
    middle = resid + attention
    normal_two, scale_two, features_two = norm_forward(middle, norm2_gain, norm2_shift)
    hidden = (
        jnp.einsum("isd,df->isf", features_two, up_full, preferred_element_type=jnp.float32)
        + up_bias
    )
    active = exact_gelu(hidden).astype(jnp.bfloat16)
    output = middle + collect(
        jnp.einsum("isf,fd->isd", active, down_full, preferred_element_type=jnp.float32)
    )
    output = output + down_bias
    saved = (
        normal_one,
        scale_one,
        features_one,
        queries,
        keys,
        values,
        logsum,
        context,
        normal_two,
        scale_two,
        features_two,
        hidden,
        active,
    )
    return (output, saved)


def layer_backward(grad_out, saved, weights, params):
    qkv_full, out_full, up_full, down_full = weights
    norm1_gain, norm1_shift, qv_bias, out_bias, norm2_gain, norm2_shift, up_bias, down_bias = params
    (
        normal_one,
        scale_one,
        features_one,
        queries,
        keys,
        values,
        logsum,
        context,
        normal_two,
        scale_two,
        features_two,
        hidden,
        active,
    ) = saved
    images, length, local_width = grad_out.shape
    grad_mlp = spread_grad(grad_out)
    down_bias_grad = token_sum(grad_out.astype(jnp.bfloat16))
    down_grad = jnp.einsum("isf,isd->fd", active, grad_mlp, preferred_element_type=jnp.float32)
    grad_active = jnp.einsum("isd,fd->isf", grad_mlp, down_full, preferred_element_type=jnp.float32)
    gelu_value, gelu_pull = jax.vjp(exact_gelu, hidden)
    grad_hidden = gelu_pull(grad_active)[0].astype(jnp.bfloat16)
    up_bias_grad = token_sum(grad_hidden)
    up_grad = jnp.einsum(
        "isd,isf->df", features_two, grad_hidden, preferred_element_type=jnp.float32
    )
    grad_normed_two = input_sum(
        jnp.einsum("isf,df->isd", grad_hidden, up_full, preferred_element_type=jnp.float32)
    )
    back_two, gain_two_grad, shift_two_grad = norm_backward(
        grad_normed_two, normal_two, scale_two, norm2_gain
    )
    grad_middle = grad_out + back_two
    grad_attention = spread_grad(grad_middle)
    out_bias_grad = token_sum(grad_middle.astype(jnp.bfloat16))
    out_grad = jnp.einsum(
        "isc,isd->cd", context, grad_attention, preferred_element_type=jnp.float32
    )
    grad_context = jnp.einsum(
        "isd,cd->isc", grad_attention, out_full, preferred_element_type=jnp.float32
    )
    grad_context = grad_context.astype(jnp.bfloat16).reshape(queries.shape)
    grad_queries, grad_keys, grad_values = lax.map(
        attend_backward, (queries, keys, values, logsum, grad_context)
    )
    stacked = jnp.stack([grad_queries, grad_keys, grad_values], 2)
    stacked = stacked.reshape(images, length, 3, local_width).astype(jnp.bfloat16)
    qv_bias_grad = jnp.stack([token_sum(stacked[:, :, 0]), token_sum(stacked[:, :, 2])])
    qkv_grad = jnp.einsum(
        "isd,istc->dtc", features_one, stacked, preferred_element_type=jnp.float32
    )
    grad_normed_one = input_sum(
        jnp.einsum("istc,dtc->isd", stacked, qkv_full, preferred_element_type=jnp.float32)
    )
    back_one, gain_one_grad, shift_one_grad = norm_backward(
        grad_normed_one, normal_one, scale_one, norm1_gain
    )
    grad_resid = grad_middle + back_one
    large = (qkv_grad, out_grad, up_grad, down_grad)
    small = (
        gain_one_grad,
        shift_one_grad,
        qv_bias_grad,
        out_bias_grad,
        gain_two_grad,
        shift_two_grad,
        up_bias_grad,
        down_bias_grad,
    )
    return (grad_resid, large, small)


def local(
    layer_input,
    cotangent,
    norm1_gain,
    norm1_shift,
    qkv_weight,
    qv_bias,
    out_weight,
    out_bias,
    norm2_gain,
    norm2_shift,
    up_weight,
    up_bias,
    down_weight,
    down_bias,
):
    section = lax.axis_index("section")
    leading = section == 0
    params = tuple(
        (
            weight_arg[0].astype(jnp.float32)
            for weight_arg in (
                norm1_gain,
                norm1_shift,
                qv_bias,
                out_bias,
                norm2_gain,
                norm2_shift,
                up_bias,
                down_bias,
            )
        )
    )
    shards = (qkv_weight[0], out_weight[0], up_weight[0], down_weight[0])

    def current():
        return (
            lax.all_gather(shards[0], "row", axis=0, tiled=True),
            lax.all_gather(shards[1], "row", axis=1, tiled=True),
            lax.all_gather(shards[2], "row", axis=0, tiled=True),
            lax.all_gather(shards[3], "row", axis=1, tiled=True),
        )

    local_input = layer_input[0]
    buffer = local_input.astype(jnp.float32)
    stash = []
    for moment in range(3):
        output, saved = layer_forward(buffer, current(), params)
        stash.append(saved)
        if moment < 2:
            outgoing = output.astype(jnp.bfloat16)
            if moment == 0:
                outgoing = jnp.where(leading, outgoing, local_input)
            arrived = partner(outgoing, "section", 0)
            buffer = arrived.astype(jnp.float32)
    final = jnp.where(leading, arrived, output.astype(jnp.bfloat16))
    local_cotangent = cotangent[0]
    gradient = local_cotangent.astype(jnp.float32)
    large_total = None
    small_total = None
    for back_step in range(3):
        moment = 2 - back_step
        valid = jnp.logical_and(moment - section >= 0, moment - section < 2)
        weights_now = current()
        saved = stash[moment]
        grad_resid, large, small = layer_backward(gradient, saved, weights_now, params)
        large = tuple((jnp.where(valid, piece, 0.0) for piece in large))
        small = tuple((jnp.where(valid, piece, 0.0) for piece in small))
        if large_total is None:
            large_total = large
            small_total = small
        else:
            large_total = tuple((total + extra for total, extra in zip(large_total, large)))
            small_total = tuple((total + extra for total, extra in zip(small_total, small)))
        if back_step < 2:
            outgoing = grad_resid.astype(jnp.bfloat16)
            if back_step == 0:
                outgoing = jnp.where(leading, local_cotangent, outgoing)
            arrived = partner(outgoing, "section", 0)
            gradient = arrived.astype(jnp.float32)
    input_grad = jnp.where(leading, grad_resid.astype(jnp.bfloat16), arrived)
    reduced = (
        lax.psum_scatter(
            large_total[0].astype(jnp.bfloat16), "row", scatter_dimension=0, tiled=True
        ).astype(jnp.float32),
        lax.psum_scatter(
            large_total[1].astype(jnp.bfloat16), "row", scatter_dimension=1, tiled=True
        ).astype(jnp.float32),
        lax.psum_scatter(
            large_total[2].astype(jnp.bfloat16), "row", scatter_dimension=0, tiled=True
        ).astype(jnp.float32),
        lax.psum_scatter(
            large_total[3].astype(jnp.bfloat16), "row", scatter_dimension=1, tiled=True
        ).astype(jnp.float32),
    )
    summed = lax.psum(small_total, "row")
    return (
        final[None],
        input_grad[None],
        summed[0][None],
        summed[1][None],
        reduced[0][None],
        summed[2][None],
        reduced[1][None],
        summed[3][None],
        summed[4][None],
        summed[5][None],
        reduced[2][None],
        summed[6][None],
        reduced[3][None],
        summed[7][None],
    )


def solution(mesh):
    placed = (
        P("section", "row", None, "col"),
        P("section", "row", None, "col"),
        P("section", "col"),
        P("section", "col"),
        P("section", "row", None, "col"),
        P("section", None, "col"),
        P("section", "col", "row"),
        P("section", "col"),
        P("section", "col"),
        P("section", "col"),
        P("section", "row", "col"),
        P("section", "col"),
        P("section", "col", "row"),
        P("section", "col"),
    )
    return jax.shard_map(
        local,
        mesh=mesh,
        in_specs=placed,
        out_specs=(
            P("section", "row", None, "col"),
            P("section", "row", None, "col"),
            P("section", "col"),
            P("section", "col"),
            P("section", "row", None, "col"),
            P("section", None, "col"),
            P("section", "col", "row"),
            P("section", "col"),
            P("section", "col"),
            P("section", "col"),
            P("section", "row", "col"),
            P("section", "col"),
            P("section", "col", "row"),
            P("section", "col"),
        ),
        check_vma=False,
    )
```

profile of v0, /device:TPU:1, one launch (start us, length us, event | category | flops | bytes accessed | tf_op | source)
XLA Modules:
  0.0 1298.6 jit_solution(13666892713140581778)
XLA Ops:
  20.6 20.7 %all-gather.1 = bf16[1,256,1024]{1,2,0:T(8,128)(2,1)S(1)} all-gather(bf16[1,256,64]{1,2,0:T(8,128)(2,1)} %param.20), channel_id=3, replica_groups=mesh['section'=2,'row'=16,'col'=4] {'row'}, dimensions={2}, use_global_device_ids=true | all-gather | bytes 557056 | tf_op jit(solution)/shard_map/all_gather | solution.py:256
  44.8 46.3 %all-gather.43.cloned.1.call-done = bf16[1,1024,3,256]{3,1,2,0:T(8,128)(2,1)} async-done(((bf16[1,64,3,256]{3,1,2,0:T(8,128)(2,1)}), bf16[1,1024,3,256]{3,1,2,0:T(8,128)(2,1)}) %all-gather.43.cloned.1.call-update) | async-done | bytes 1572880 | tf_op jit(solution)/shard_map/all_gather | solution.py:255
  105.2 21.0 %reduce-scatter.19.cloned.1.call-done = bf16[1,577,256]{2,1,0:T(8,128)(2,1)} async-done(((bf16[1,577,1024]{2,1,0:T(8,128)(2,1)}), bf16[1,577,256]{2,1,0:T(8,128)(2,1)}) %reduce-scatter.19.cloned.1.call-update) | async-done | bytes 295440 | tf_op jit(solution)/shard_map/reduce_scatter | solution.py:43
  135.5 37.6 %all-gather.45.cloned.1.call-done = bf16[1,1024,1024]{2,1,0:T(8,128)(2,1)} async-done(((bf16[1,64,1024]{2,1,0:T(8,128)(2,1)}), bf16[1,1024,1024]{2,1,0:T(8,128)(2,1)}) %all-gather.45.cloned.1.call-update) | async-done | bytes 2097168 | tf_op jit(solution)/shard_map/all_gather | solution.py:257
  173.1 24.5 %all-gather.23.cloned.1.call-done = bf16[1,577,1024]{2,1,0:T(8,128)(2,1)} async-done(((bf16[1,577,256]{2,1,0:T(8,128)(2,1)}), bf16[1,577,1024]{2,1,0:T(8,128)(2,1)}) %all-gather.23.cloned.1.call-update) | async-done | bytes 1181712 | tf_op jit(solution)/shard_map/all_gather | solution.py:26
  207.1 38.1 %all-gather.47.cloned.1.call-done = bf16[1,1024,1024]{1,2,0:T(8,128)(2,1)} async-done(((bf16[1,1024,64]{1,2,0:T(8,128)(2,1)}), bf16[1,1024,1024]{1,2,0:T(8,128)(2,1)}) %all-gather.47.cloned.1.call-update) | async-done | bytes 2097168 | tf_op jit(solution)/shard_map/all_gather | solution.py:258
  249.4 21.6 %reduce-scatter.21.cloned.1.call-done = bf16[1,577,256]{2,1,0:T(8,128)(2,1)} async-done(((bf16[1,577,1024]{2,1,0:T(8,128)(2,1)}), bf16[1,577,256]{2,1,0:T(8,128)(2,1)}) %reduce-scatter.21.cloned.1.call-update) | async-done | bytes 295440 | tf_op jit(solution)/shard_map/reduce_scatter | solution.py:43
  289.7 23.1 %all-gather.25.cloned.1.call-done = bf16[1,577,1024]{2,1,0:T(8,128)(2,1)} async-done(((bf16[1,577,256]{2,1,0:T(8,128)(2,1)}), bf16[1,577,1024]{2,1,0:T(8,128)(2,1)}) %all-gather.25.cloned.1.call-update) | async-done | bytes 1181712 | tf_op jit(solution)/shard_map/all_gather | solution.py:26
  328.2 22.4 %reduce-scatter.23.cloned.1.call-done = bf16[1,577,256]{2,1,0:T(8,128)(2,1)} async-done(((bf16[1,577,1024]{2,1,0:T(8,128)(2,1)}), bf16[1,577,256]{2,1,0:T(8,128)(2,1)}) %reduce-scatter.23.cloned.1.call-update) | async-done | bytes 295440 | tf_op jit(solution)/shard_map/reduce_scatter | solution.py:43
  359.7 23.4 %all-gather.27.cloned.1.call-done = bf16[1,577,1024]{2,1,0:T(8,128)(2,1)} async-done(((bf16[1,577,256]{2,1,0:T(8,128)(2,1)}), bf16[1,577,1024]{2,1,0:T(8,128)(2,1)}) %all-gather.27.cloned.1.call-update) | async-done | bytes 1181712 | tf_op jit(solution)/shard_map/all_gather | solution.py:26
  396.3 22.4 %reduce-scatter.25.cloned.1.call-done = bf16[1,577,256]{2,1,0:T(8,128)(2,1)} async-done(((bf16[1,577,1024]{2,1,0:T(8,128)(2,1)}), bf16[1,577,256]{2,1,0:T(8,128)(2,1)}) %reduce-scatter.25.cloned.1.call-update) | async-done | bytes 295440 | tf_op jit(solution)/shard_map/reduce_scatter | solution.py:43
  437.3 23.1 %all-gather.29.cloned.1.call-done = bf16[1,577,1024]{2,1,0:T(8,128)(2,1)} async-done(((bf16[1,577,256]{2,1,0:T(8,128)(2,1)}), bf16[1,577,1024]{2,1,0:T(8,128)(2,1)}) %all-gather.29.cloned.1.call-update) | async-done | bytes 1181712 | tf_op jit(solution)/shard_map/all_gather | solution.py:26
  481.1 22.4 %reduce-scatter.27.cloned.1.call-done = bf16[1,577,256]{2,1,0:T(8,128)(2,1)} async-done(((bf16[1,577,1024]{2,1,0:T(8,128)(2,1)}), bf16[1,577,256]{2,1,0:T(8,128)(2,1)}) %reduce-scatter.27.cloned.1.call-update) | async-done | bytes 295440 | tf_op jit(solution)/shard_map/reduce_scatter | solution.py:43
  512.9 23.2 %all-gather.31.cloned.1.call-done = bf16[1,577,1024]{2,1,0:T(8,128)(2,1)} async-done(((bf16[1,577,256]{2,1,0:T(8,128)(2,1)}), bf16[1,577,1024]{2,1,0:T(8,128)(2,1)}) %all-gather.31.cloned.1.call-update) | async-done | bytes 1181712 | tf_op jit(solution)/shard_map/all_gather | solution.py:26
  536.2 9.6 multiply_convert_fusion.3
  545.8 15.1 %all-gather.49.cloned.1.call-done = bf16[1,1,577,1024]{3,2,1,0:T(8,128)(2,1)} async-done(((bf16[1,1,577,256]{3,2,1,0:T(8,128)(2,1)}), bf16[1,1,577,1024]{3,2,1,0:T(8,128)(2,1)}) %all-gather.49.cloned.1.call-update) | async-done | bytes 1181712 | tf_op jit(solution)/shard_map/all_gather | solution.py:49
  570.2 22.4 %reduce-scatter.31.cloned.1.call-done = bf16[1,577,256]{2,1,0:T(8,128)(2,1)} async-done(((bf16[1,577,1024]{2,1,0:T(8,128)(2,1)}), bf16[1,577,256]{2,1,0:T(8,128)(2,1)}) %reduce-scatter.31.cloned.1.call-update) | async-done | bytes 295440 | tf_op jit(solution)/shard_map/reduce_scatter | solution.py:53
  602.0 23.7 %all-gather.33.cloned.1.call-done = bf16[1,577,1024]{2,1,0:T(8,128)(2,1)} async-done(((bf16[1,577,256]{2,1,0:T(8,128)(2,1)}), bf16[1,577,1024]{2,1,0:T(8,128)(2,1)}) %all-gather.33.cloned.1.call-update) | async-done | bytes 1181712 | tf_op jit(solution)/shard_map/all_gather | solution.py:49
  657.9 17.9 %reduce-scatter.33.cloned.1.call-done = bf16[1,577,256]{2,1,0:T(8,128)(2,1)} async-done(((bf16[1,577,1024]{2,1,0:T(8,128)(2,1)}), bf16[1,577,256]{2,1,0:T(8,128)(2,1)}) %reduce-scatter.33.cloned.1.call-update) | async-done | bytes 295440 | tf_op jit(solution)/shard_map/reduce_scatter | solution.py:53
  682.6 17.5 %reduce-scatter.29.cloned.1.call-done = bf16[1,577,256]{2,1,0:T(8,128)(2,1)} async-done(((bf16[1,577,1024]{2,1,0:T(8,128)(2,1)}), bf16[1,577,256]{2,1,0:T(8,128)(2,1)}) %reduce-scatter.29.cloned.1.call-update) | async-done | bytes 295440 | tf_op jit(solution)/shard_map/reduce_scatter | solution.py:43
  713.8 23.2 %all-gather.35.cloned.1.call-done = bf16[1,577,1024]{2,1,0:T(8,128)(2,1)} async-done(((bf16[1,577,256]{2,1,0:T(8,128)(2,1)}), bf16[1,577,1024]{2,1,0:T(8,128)(2,1)}) %all-gather.35.cloned.1.call-update) | async-done | bytes 1181712 | tf_op jit(solution)/shard_map/all_gather | solution.py:49
  746.3 22.4 %reduce-scatter.35.cloned.1.call-done = bf16[1,577,256]{2,1,0:T(8,128)(2,1)} async-done(((bf16[1,577,1024]{2,1,0:T(8,128)(2,1)}), bf16[1,577,256]{2,1,0:T(8,128)(2,1)}) %reduce-scatter.35.cloned.1.call-update) | async-done | bytes 295440 | tf_op jit(solution)/shard_map/reduce_scatter | solution.py:53
  778.1 24.0 %all-gather.37.cloned.1.call-done = bf16[1,577,1024]{2,1,0:T(8,128)(2,1)} async-done(((bf16[1,577,256]{2,1,0:T(8,128)(2,1)}), bf16[1,577,1024]{2,1,0:T(8,128)(2,1)}) %all-gather.37.cloned.1.call-update) | async-done | bytes 1181712 | tf_op jit(solution)/shard_map/all_gather | solution.py:49
  821.9 22.2 %reduce-scatter.37.cloned.1.call-done = bf16[1,577,256]{2,1,0:T(8,128)(2,1)} async-done(((bf16[1,577,1024]{2,1,0:T(8,128)(2,1)}), bf16[1,577,256]{2,1,0:T(8,128)(2,1)}) %reduce-scatter.37.cloned.1.call-update) | async-done | bytes 295440 | tf_op jit(solution)/shard_map/reduce_scatter | solution.py:53
  861.8 24.7 %all-gather.39.cloned.1.call-done = bf16[1,577,1024]{2,1,0:T(8,128)(2,1)} async-done(((bf16[1,577,256]{2,1,0:T(8,128)(2,1)}), bf16[1,577,1024]{2,1,0:T(8,128)(2,1)}) %all-gather.39.cloned.1.call-update) | async-done | bytes 1181712 | tf_op jit(solution)/shard_map/all_gather | solution.py:49
  895.9 22.4 %reduce-scatter.39.cloned.1.call-done = bf16[1,577,256]{2,1,0:T(8,128)(2,1)} async-done(((bf16[1,577,1024]{2,1,0:T(8,128)(2,1)}), bf16[1,577,256]{2,1,0:T(8,128)(2,1)}) %reduce-scatter.39.cloned.1.call-update) | async-done | bytes 295440 | tf_op jit(solution)/shard_map/reduce_scatter | solution.py:53
  993.2 35.9 %reduce-scatter.49.cloned.1.call-done = bf16[64,1024]{1,0:T(8,128)(2,1)} async-done(((bf16[1024,1024]{1,0:T(8,128)(2,1)}), bf16[64,1024]{1,0:T(8,128)(2,1)}) %reduce-scatter.49.cloned.1.call-update) | async-done | bytes 131088
  1031.1 75.1 %reduce-scatter.47.cloned.1.call-done = bf16[64,1024]{1,0:T(8,128)(2,1)} async-done(((bf16[1024,1024]{1,0:T(8,128)(2,1)}), bf16[64,1024]{1,0:T(8,128)(2,1)}) %reduce-scatter.47.cloned.1.call-update) | async-done | bytes 131088 | tf_op jit(solution)/shard_map/reduce_scatter | solution.py:306
  1107.8 73.5 %reduce-scatter.45.cloned.1.call-done = bf16[256,64]{0,1:T(8,128)(2,1)} async-done(((bf16[256,1024]{0,1:T(8,128)(2,1)}), bf16[256,64]{0,1:T(8,128)(2,1)}) %reduce-scatter.45.cloned.1.call-update) | async-done | bytes 32784 | tf_op jit(solution)/shard_map/reduce_scatter | solution.py:303
  1182.7 23.0 %reduce-scatter.41.cloned.1.call-done = bf16[1,577,256]{2,1,0:T(8,128)(2,1)} async-done(((bf16[1,577,1024]{2,1,0:T(8,128)(2,1)}), bf16[1,577,256]{2,1,0:T(8,128)(2,1)}) %reduce-scatter.41.cloned.1.call-update) | async-done | bytes 295440 | tf_op jit(solution)/shard_map/reduce_scatter | solution.py:53
  1207.2 60.8 %all-reduce = (f32[1,256]{1,0:T(1,128)}, f32[1,256]{1,0:T(1,128)}, f32[1,2,256]{2,1,0:T(2,128)}, f32[1,256]{1,0:T(1,128)}, f32[1,256]{1,0:T(1,128)}, /*index=5*/...) all-reduce(f32[1,256]{1,0:T(1,128)S(1)} %bitcast.484, ...), channel_id=1, replica_groups=mesh['section'=2,'row'=16,'col'=4] {'row'}, use_global_device_ids=true, to_apply=%region_72.73 | all-reduce | flops 3072 | bytes 24576 | tf_op jit(solution)/shard_map/psum | solution.py:313
  1268.0 19.2 %all-reduce.1 = (f32[1,577]{1,0:T(1,128)S(1)}, f32[1,577]{1,0:T(1,128)S(1)}) all-reduce(f32[1,577]{1,0:T(1,128)S(1)} %reduce_sum.620, f32[1,577]{1,0:T(1,128)S(1)} %reduce_sum.618), channel_id=1, replica_groups=mesh['section'=2,'row'=16,'col'=4] {'col'}, use_global_device_ids=true, to_apply=%region_68.69 | all-reduce | flops 1154 | bytes 9232 | tf_op jit(solution)/shard_map/psum | solution.py:35
  (452 shorter events, 379.0 us)
Async XLA Ops:
  7.2 37.6 %all-gather.21.cloned.1.call-start = ((), (), s32[]{:S(2)}) async-start(), calls=%async_computation.16 | async-start | bytes 1495040 | tf_op jit(solution)/shard_map/all_gather | solution.py:26
  18.9 72.2 %all-gather.43.cloned.1.call-start = ((), (), s32[]{:S(2)}) async-start(), calls=%async_computation.42 | async-start | bytes 1671168 | tf_op jit(solution)/shard_map/all_gather | solution.py:255
  19.7 106.5 %reduce-scatter.19.cloned.1.call-start = ((), (), s32[]{:S(2)}) async-start(), calls=%async_computation.17 | async-start | bytes 1495040 | tf_op jit(solution)/shard_map/reduce_scatter | solution.py:43
  104.5 68.7 %all-gather.45.cloned.1.call-start = ((), (), s32[]{:S(2)}) async-start(), calls=%async_computation.43 | async-start | bytes 2228224 | tf_op jit(solution)/shard_map/all_gather | solution.py:257
  105.1 92.6 %all-gather.23.cloned.1.call-start = ((), (), s32[]{:S(2)}) async-start(), calls=%async_computation.18 | async-start | bytes 1495040 | tf_op jit(solution)/shard_map/all_gather | solution.py:26
  134.7 110.5 %all-gather.47.cloned.1.call-start = ((), (), s32[]{:S(2)}) async-start(), calls=%async_computation.44 | async-start | bytes 2228224 | tf_op jit(solution)/shard_map/all_gather | solution.py:258
  135.3 135.8 %reduce-scatter.21.cloned.1.call-start = ((), (), s32[]{:S(2)}) async-start(), calls=%async_computation.19 | async-start | bytes 1495040 | tf_op jit(solution)/shard_map/reduce_scatter | solution.py:43
  249.3 63.5 %all-gather.25.cloned.1.call-start = ((), (), s32[]{:S(2)}) async-start(), calls=%async_computation.20 | async-start | bytes 1495040 | tf_op jit(solution)/shard_map/all_gather | solution.py:26
  272.2 10.0 collective-permute-start
  289.6 61.0 %reduce-scatter.23.cloned.1.call-start = ((), (), s32[]{:S(2)}) async-start(), calls=%async_computation.21 | async-start | bytes 1495040 | tf_op jit(solution)/shard_map/reduce_scatter | solution.py:43
  328.1 55.1 %all-gather.27.cloned.1.call-start = ((), (), s32[]{:S(2)}) async-start(), calls=%async_computation.22 | async-start | bytes 1495040 | tf_op jit(solution)/shard_map/all_gather | solution.py:26
  359.3 59.4 %reduce-scatter.25.cloned.1.call-start = ((), (), s32[]{:S(2)}) async-start(), calls=%async_computation.23 | async-start | bytes 1495040 | tf_op jit(solution)/shard_map/reduce_scatter | solution.py:43
  396.2 64.2 %all-gather.29.cloned.1.call-start = ((), (), s32[]{:S(2)}) async-start(), calls=%async_computation.24 | async-start | bytes 1495040 | tf_op jit(solution)/shard_map/all_gather | solution.py:26
  437.3 66.3 %reduce-scatter.27.cloned.1.call-start = ((), (), s32[]{:S(2)}) async-start(), calls=%async_computation.25 | async-start | bytes 1495040 | tf_op jit(solution)/shard_map/reduce_scatter | solution.py:43
  481.1 55.1 %all-gather.31.cloned.1.call-start = ((), (), s32[]{:S(2)}) async-start(), calls=%async_computation.26 | async-start | bytes 1495040 | tf_op jit(solution)/shard_map/all_gather | solution.py:26
  512.1 48.8 %all-gather.49.cloned.1.call-start = ((), (), s32[]{:S(2)}) async-start(), calls=%async_computation.45 | async-start | bytes 1495040 | tf_op jit(solution)/shard_map/all_gather | solution.py:49
  512.7 79.9 %reduce-scatter.31.cloned.1.call-start = ((), (), s32[]{:S(2)}) async-start(), calls=%async_computation.28 | async-start | bytes 1495040 | tf_op jit(solution)/shard_map/reduce_scatter | solution.py:53
  570.2 55.6 %all-gather.33.cloned.1.call-start = ((), (), s32[]{:S(2)}) async-start(), calls=%async_computation.29 | async-start | bytes 1495040 | tf_op jit(solution)/shard_map/all_gather | solution.py:49
  601.8 74.0 %reduce-scatter.33.cloned.1.call-start = ((), (), s32[]{:S(2)}) async-start(), calls=%async_computation.30 | async-start | bytes 1495040 | tf_op jit(solution)/shard_map/reduce_scatter | solution.py:53
  653.3 46.9 %reduce-scatter.29.cloned.1.call-start = ((), (), s32[]{:S(2)}) async-start(), calls=%async_computation.27 | async-start | bytes 1495040 | tf_op jit(solution)/shard_map/reduce_scatter | solution.py:43
  657.8 79.2 %all-gather.35.cloned.1.call-start = ((), (), s32[]{:S(2)}) async-start(), calls=%async_computation.31 | async-start | bytes 1495040 | tf_op jit(solution)/shard_map/all_gather | solution.py:49
  713.3 55.4 %reduce-scatter.35.cloned.1.call-start = ((), (), s32[]{:S(2)}) async-start(), calls=%async_computation.32 | async-start | bytes 1495040 | tf_op jit(solution)/shard_map/reduce_scatter | solution.py:53
  746.2 55.8 %all-gather.37.cloned.1.call-start = ((), (), s32[]{:S(2)}) async-start(), calls=%async_computation.33 | async-start | bytes 1495040 | tf_op jit(solution)/shard_map/all_gather | solution.py:49
  778.0 66.1 %reduce-scatter.37.cloned.1.call-start = ((), (), s32[]{:S(2)}) async-start(), calls=%async_computation.34 | async-start | bytes 1495040 | tf_op jit(solution)/shard_map/reduce_scatter | solution.py:53
  821.6 64.9 %all-gather.39.cloned.1.call-start = ((), (), s32[]{:S(2)}) async-start(), calls=%async_computation.35 | async-start | bytes 1495040 | tf_op jit(solution)/shard_map/all_gather | solution.py:49
  861.8 56.6 %reduce-scatter.39.cloned.1.call-start = ((), (), s32[]{:S(2)}) async-start(), calls=%async_computation.36 | async-start | bytes 1495040 | tf_op jit(solution)/shard_map/reduce_scatter | solution.py:53
  895.9 57.6 %all-gather.41.cloned.1.call-start = ((), (), s32[]{:S(2)}) async-start(), calls=%async_computation.37 | async-start | bytes 1495040 | tf_op jit(solution)/shard_map/all_gather | solution.py:49
  927.3 101.7 %reduce-scatter.49.cloned.1.call-start = ((), (), s32[]{:S(2)}) async-start(), calls=%async_computation.46 | async-start | bytes 2228224
  940.3 165.9 %reduce-scatter.47.cloned.1.call-start = ((), (), s32[]{:S(2)}) async-start(), calls=%async_computation.41 | async-start | bytes 2228224 | tf_op jit(solution)/shard_map/reduce_scatter | solution.py:306
  949.3 232.0 %reduce-scatter.45.cloned.1.call-start = ((), (), s32[]{:S(2)}) async-start(), calls=%async_computation.40 | async-start | bytes 557056 | tf_op jit(solution)/shard_map/reduce_scatter | solution.py:303
  966.1 239.6 %reduce-scatter.41.cloned.1.call-start = ((), (), s32[]{:S(2)}) async-start(), calls=%async_computation.38 | async-start | bytes 1495040 | tf_op jit(solution)/shard_map/reduce_scatter | solution.py:53
  985.1 304.7 %reduce-scatter.43.cloned.1.call-start = ((), (), s32[]{:S(2)}) async-start(), calls=%async_computation.39 | async-start | bytes 1671168 | tf_op jit(solution)/shard_map/reduce_scatter | solution.py:300
  (93 other events, 2152.7 us)
Sparse Core Ops, SparseCore 0:
  19.0 25.6 all-gather.20
  47.0 44.1 all-gather.42
  104.6 21.5 reduce-scatter.18
  128.4 44.6 all-gather.44
  175.3 22.3 all-gather.22
  199.9 45.2 all-gather.46
  249.5 21.5 reduce-scatter.20
  289.7 23.0 all-gather.24
  328.2 22.2 reduce-scatter.22
  359.4 23.7 all-gather.26
  396.3 22.3 reduce-scatter.24
  437.4 22.9 all-gather.28
  481.2 22.2 reduce-scatter.26
  512.3 23.8 all-gather.30
  537.8 23.0 all-gather.48
  570.3 22.2 reduce-scatter.30
  601.9 23.8 all-gather.32
  653.4 22.2 reduce-scatter.32
  678.3 21.7 reduce-scatter.28
  713.5 23.5 all-gather.34
  746.3 22.2 reduce-scatter.34
  778.1 23.8 all-gather.36
  821.8 22.2 reduce-scatter.36
  861.9 24.6 all-gather.38
  896.0 22.3 reduce-scatter.38
  927.5 23.9 all-gather.40
  954.9 74.1 reduce-scatter.48
  1032.3 73.7 reduce-scatter.46
  1109.7 71.5 reduce-scatter.44
  1183.6 22.0 reduce-scatter.40
  1209.3 72.9 reduce-scatter.42
where the time goes:
time: 1310 us; the launch traced here: 1300 us
  waiting for transfers between devices  827 us (63%)
  matrix products  182 us (14%)
  blocking collectives  163 us (12%)
  other arithmetic  53.3 us (4%)
  local copies, waits for them, and re-layouts  43 us (3%)
  between operations  16.7 us (1%)
  starting transfers between devices  13.2 us (1%)
    reduce_scatter x6, waiting for transfers between devices, input_sum(): lax.psum_scatter(partial_sum.astype(jnp.bfloat16), 'col', scatter_dimensi...  130 us
    reduce_scatter x6, waiting for transfers between devices, collect(): lax.psum_scatter(partial_sum.astype(jnp.bfloat16), 'col', scatter_dimensi...  127 us
    all_gather x6, waiting for transfers between devices, norm_forward(): lax.all_gather((normal * gain + shift).astype(jnp.bfloat16), 'col', axis=...  121 us
    all_gather x6, waiting for transfers between devices, spread_grad(): return lax.all_gather(grad.astype(jnp.bfloat16), 'col', axis=2, tiled=True)  111 us
    reduce_scatter x1, waiting for transfers between devices, local(): lax.psum_scatter(large_total[2].astype(jnp.bfloat16), 'row', scatter_dime...  75.1 us
    reduce_scatter x1, waiting for transfers between devices, local(): lax.psum_scatter(large_total[1].astype(jnp.bfloat16), 'row', scatter_dime...  73.5 us
    psum x1, blocking collectives, local(): summed = lax.psum(small_total, 'row')  60.8 us
    all_gather x1, waiting for transfers between devices, current(): lax.all_gather(shards[0], 'row', axis=0, tiled=True)  46.3 us
  transfers between devices with their start and end apart: 35, of which 33 were waited for; matrix products, arithmetic and copies ran while one was open for 8% of the time, Pallas kernels for 0%

commit v1 on v0

v1 whole, which is shorter than its diff:
```python
import functools

import jax
import jax.numpy as jnp
from jax import lax
from jax.experimental import pallas as pl
from jax.experimental.pallas import tpu as pltpu
from jax.sharding import PartitionSpec as P

HD = 64
EPS = 1e-06
TOKENS = 577
HALF = 304
ROWS = 2 * HALF
D = 1024
BF16 = jnp.bfloat16
F32 = jnp.float32
VMEM_LIMIT = 24 * 1024 * 1024


def swap(value, axis, mask):
    return lax.ppermute(value, axis, [(i, i ^ mask) for i in range(lax.axis_size(axis))])


def after(value, *marks):
    return lax.optimization_barrier((value,) + marks)[0]


def dot(left, right, left_dim, right_dim):
    return lax.dot_general(
        left, right, (((left_dim,), (right_dim,)), ((), ())), preferred_element_type=F32
    )


class Place:
    def __init__(self):
        self.section = lax.axis_index("section")
        col = lax.axis_index("col")
        self.y = col // 2
        self.core = col % 2
        self.col = col


UNIT = {"x": 4, "z": 1}
MASKS = (3, 1)
LIGHT = {"x": "z", "z": "x"}


def ring_blocks(name):
    row = lax.axis_index("row")
    here = row // 4 if name == "x" else row % 4
    first, second = MASKS
    return here, here ^ first, here ^ second, here ^ first ^ second


def call(kernel, outs, ins, name, scratch=()):
    return pl.pallas_call(
        kernel,
        out_shape=[jax.ShapeDtypeStruct(*out) for out in outs],
        scratch_shapes=list(scratch),
        compiler_params=pltpu.CompilerParams(vmem_limit_bytes=VMEM_LIMIT),
        cost_estimate=pl.CostEstimate(flops=0, bytes_accessed=0, transcendentals=0),
        name=name,
    )(*ins)


def place_kernel(name, dim, *refs):
    *pieces, out = refs
    for piece, block in zip(pieces, ring_blocks(name)):
        if dim == 0:
            out[block] = piece[...]
        else:
            out[:, block] = piece[...]


def place_halves_kernel(name, dim, own, near, far, low, high, out):
    blocks = ring_blocks(name)
    half = low.shape[0]
    for piece, block in zip((own, near, far), blocks):
        if dim == 0:
            out[block] = piece[...]
        else:
            out[:, block] = piece[...]
    if dim == 0:
        out[blocks[3], :half] = low[...]
        out[blocks[3], half:] = high[...]
    else:
        out[:half, blocks[3]] = low[...]
        out[half:, blocks[3]] = high[...]


def ring_gather(value, name, dim, *middle):
    first, second = (mask * UNIT[name] for mask in MASKS)
    near = swap(value, "row", first)
    far = swap(value, "row", second)
    both = swap(after(near, *middle) if middle else near, "row", second)
    shape = value.shape[:dim] + (4,) + value.shape[dim:]
    kernel = functools.partial(place_kernel, name, dim)
    return call(kernel, [(shape, BF16)], (value, near, far, both), "place_blocks")[0]


def gather_light(shard, stream, *middle):
    part = ring_gather(shard, LIGHT[stream], 0, *middle)
    return part.reshape(256, shard.shape[1]) if stream == "x" else part


class Heavy:
    def __init__(self, part, stream):
        self.part, self.stream = part, stream
        self.first, self.second = (mask * UNIT[stream] for mask in MASKS)
        self.near = swap(part, "row", self.first)
        self.far = swap(part, "row", self.second)

    def finish(self, *marks):
        near, far = lax.optimization_barrier((self.near, self.far) + marks)[:2]
        half = near.shape[0] // 2
        self.sent = (near[:half], far[half:])
        self.low = low = swap(self.sent[0], "row", self.second)
        self.high = high = swap(self.sent[1], "row", self.first)
        dim = 0 if self.stream == "x" else 1
        shape = near.shape[:dim] + (4,) + near.shape[dim:]
        kernel = functools.partial(place_halves_kernel, self.stream, dim)
        ins = (self.part, near, far, low, high)
        return call(kernel, [(shape, BF16)], ins, "place_blocks")[0].reshape(D, -1)


def pack_kernel(*refs):
    *ins, out = refs
    for index, value in enumerate(ins[:6]):
        out[index : index + 1] = value[...]
    out[6:8] = ins[6][0]
    for index in range(4):
        out[8 + index : 9 + index] = ins[7][:, 256 * index : 256 * index + 256]
    out[12:16] = jnp.zeros((4, 256), BF16)


def join(refs, out):
    start = 0
    for ref in refs:
        out[start : start + ref.shape[0]] = ref[...]
        start += ref.shape[0]


def grads_kernel(x_widths, z_widths, done, ride, *refs):
    refs = list(refs)
    tile, left = refs.pop(), refs.pop()
    first = 3 * len(x_widths + z_widths)
    extra = refs[first : first + 10]
    if ride:
        rows = refs[first + 10 * done][...].astype(BF16)
        for out in refs[-10:][3:5]:
            out[128:144] = rows[:, :512]
            out[144:160] = rows[:, 512:]

    def blocks(stream, width, store):
        one, other, right = (refs.pop(0) for _ in range(3))
        join((one, other), left)
        for low in range(0, width, 256):
            columns = slice(low, low + 256)
            if stream == "x":
                for index, block in enumerate(ring_blocks("x")):
                    at = pl.ds(pl.multiple_of(block * 256, 256), 256)
                    store(index, None, low, dot(left[:, at], right[:, columns], 0, 0))
                continue
            for x in range(4):
                tile[...] = dot(left[:, 256 * x : 256 * x + 256], right[:, columns], 0, 0)
                for index, block in enumerate(ring_blocks("z")):
                    rows = pl.ds(pl.multiple_of(block * 64, 64), 64)
                    store(index, x, low, tile[rows, :])

    outs = refs[-10:]
    for stream, widths, out in (("x", x_widths, outs[:5]), ("z", z_widths, outs[5:])):
        start = 0
        for width in widths:

            def store(index, x, low, value):
                columns = slice(start + low, start + low + 256)
                value = value.astype(BF16)
                if index < 3:
                    if x is None:
                        out[index][:, columns] = value
                    else:
                        out[index][x, :, columns] = value
                elif x is None:
                    out[3][:128, columns] = value[:128]
                    out[4][:128, columns] = value[128:]
                else:
                    out[3 + x // 2][x % 2, :, columns] = value

            blocks(stream, width, store)
            start += width
        for index in range(5 if done else 0):
            out[index][..., start:] = extra[(0 if stream == "x" else 5) + index][...]


def weight_grads(x_parts, z_parts, name, done=(), ride=()):
    ins, widths = [], ([], [])
    extra = done[0].shape[-1] if done else 0
    for index, parts in enumerate((x_parts, z_parts)):
        for halves, right in parts:
            ins += [*halves, right]
            widths[index].append(right.shape[1])
    outs = []
    for lead, total in (((256,), sum(widths[0]) + extra), ((4, 64), sum(widths[1]) + extra)):
        half = (lead[0] // 2,) + lead[1:]
        if ride and len(lead) == 1:
            half = (half[0] + 32,)
        outs += [lead + (total,)] * 3 + [half + (total,)] * 2
    outs = call(
        functools.partial(grads_kernel, tuple(widths[0]), tuple(widths[1]), bool(done), bool(ride)),
        [(out, BF16) for out in outs],
        ins + list(done) + list(ride),
        name,
        scratch=(pltpu.VMEM((ROWS, D), BF16), pltpu.VMEM((256, 256), F32)),
    )
    return tuple(outs)


def rider(rows):
    if rows.shape[0] == 32:
        return jnp.concatenate([rows[:16], rows[16:]], 1)
    return rows[:, :D]


def join_kernel(ride, *refs):
    refs = list(refs)
    part_out = refs.pop() if ride else None
    own_out, near_out, far_out = refs[-3:]
    ins = refs[: -4 if ride else -3]
    start = 0
    for index in range(0, len(ins), 5):
        own, near, far, low, high = ins[index : index + 5]
        size = near.shape[0]
        half = size // 2
        columns = slice(start, start + own.shape[-1])
        own_out[..., columns] = own[...]
        near_out[:half, ..., columns] = (
            near[:half].astype(F32) + low[:half].astype(F32)
        ).astype(BF16)
        near_out[half:size, ..., columns] = near[half:]
        far_out[:half, ..., columns] = far[:half]
        far_out[half:, ..., columns] = (far[half:].astype(F32) + high[:half].astype(F32)).astype(BF16)
        if low.shape[0] > half:
            passed = rider(low[half:])
            near_out[size:, :D] = passed
            near_out[size:, D:] = jnp.zeros((16, near_out.shape[1] - D), BF16)
            part_out[...] = (
                refs[-4][...] + passed.astype(F32) + rider(high[half:]).astype(F32)
            )
        start += own.shape[-1]


def split_kernel(stream, groups, ride, *refs):
    refs = list(refs)
    total = refs.pop()
    sums_out = refs.pop() if ride else None
    own, near, far, low, high = refs[-5:]
    ins = refs[:-5]
    if ride:
        sums = ins.pop()[...] + rider(ins[1][256:]).astype(F32)
        sums_out[...] = sums
        for out in (low, high):
            out[32:, :D] = sums.astype(BF16)
            out[32:, D:] = jnp.zeros((16, out.shape[1] - D), BF16)
    blocks = ring_blocks(LIGHT[stream])
    start = 0
    for count in groups:
        parts, ins = ins[:count], ins[count:]
        width = parts[0].shape[-1]
        value = parts[0][...].astype(F32)
        for part in parts[1:]:
            value += part[: value.shape[0]].astype(F32)
        total[..., :width] = value
        columns = slice(start, start + width)
        for out, block in zip((own, near, far, None), blocks):
            if stream == "x":
                rows = pl.ds(pl.multiple_of(block * 64, 64), 64)
                value = total[rows, :width].astype(BF16)
            else:
                value = total[block, :, :width].astype(BF16)
            if out is None:
                low[:32, columns] = value[:32]
                high[:32, columns] = value[32:]
            else:
                out[:, columns] = value
        start += width


def split(stream, groups, ride):
    width = sum(group[0].shape[-1] for group in groups)
    widest = max(group[0].shape[-1] for group in groups)
    half = 48 if ride else 32
    return call(
        functools.partial(split_kernel, stream, tuple(len(group) for group in groups), bool(ride)),
        [((rows, width), BF16) for rows in (64, 64, 64, half, half)] + [((16, D), F32)] * len(ride),
        [part for group in groups for part in group] + list(ride),
        "split_blocks",
        scratch=(pltpu.VMEM(groups[0][0].shape[:-1] + (widest,), F32),),
    )


def over_far(name, value):
    return swap(value, "row", MASKS[1] * UNIT[name])


def over_near(name, value):
    return swap(value, "row", MASKS[0] * UNIT[name])


class Ring:
    def __init__(self, name, own, near, far, low, high):
        self.name, self.own, self.near, self.far = name, own, near, far
        self.low, self.high = over_far(name, low), over_near(name, high)

    def finish(self, *marks, beside=(), ride=()):
        rings = (self,) + tuple(beside)
        ins = [part for ring in rings for part in (ring.own, ring.near, ring.far)]
        ins = lax.optimization_barrier((*ins, *marks))[: len(ins)]
        shape = self.own.shape[:-1] + (sum(ring.own.shape[-1] for ring in rings),)
        wide = (shape[0] + 16 * len(ride),) + shape[1:]
        ins = [
            part
            for index, ring in enumerate(rings)
            for part in (*ins[3 * index : 3 * index + 3], ring.low, ring.high)
        ]
        outs = [(shape, BF16), (wide, BF16), (shape, BF16)] + [((16, D), F32)] * len(ride)
        kernel = functools.partial(join_kernel, bool(ride))
        own, near, far, *self.ride = call(kernel, outs, ins + list(ride), "join_blocks")
        self.sent = near, far
        return own, over_near(self.name, near), over_far(self.name, far)


def light_ring(stream, *groups, ride=()):
    own, near, far, low, high, *ride = split(stream, groups, ride)
    ring = Ring(LIGHT[stream], own, near, far, low, high)
    ring.riding = ride
    return ring


def light_sum(ring, *marks):
    own, near, far = ring.finish(*marks, ride=ring.riding)
    total = own.astype(F32) + near[:64].astype(F32) + far.astype(F32)
    if not ring.riding:
        return total
    return total, ring.ride[0] + near[64:, :D].astype(F32)


def column_sums(own, other):
    return jnp.sum(own[...].astype(F32), 0, keepdims=True) + jnp.sum(
        other[...].astype(F32), 0, keepdims=True
    )


def head_mask(head):
    lane = lax.broadcasted_iota(jnp.int32, (1, 256), 1)
    return lane // HD == head


QUERY_CUTS = ((0, HALF), (HALF, ROWS))
GRAD_CUTS = ((0, 256), (256, 512), (512, ROWS))
HALVES = (slice(0, HALF), slice(HALF, ROWS))


def attend_forward_kernel(
    own, other, weights, bias, qv_bias, q_out, k_out, v_out, context, send, mine
):
    for rows, part in zip(HALVES, (own, other)):
        mixed = dot(part[...], weights[:, :768], 1, 0)
        q_out[rows] = (mixed[:, :256] + qv_bias[:, :256]).astype(BF16)
        k_out[rows] = mixed[:, 256:512].astype(BF16)
        v_out[rows] = (mixed[:, 512:] + qv_bias[:, 256:]).astype(BF16)
    for low, high in QUERY_CUTS:
        total = jnp.zeros((high - low, 256), F32)
        for head in range(4):
            mask = head_mask(head)
            queries = jnp.where(mask, q_out[low:high].astype(F32) * 0.125, 0.0).astype(BF16)
            scores = dot(queries, k_out[...], 1, 1) + bias[...]
            raised = jnp.exp(scores - jnp.max(scores, -1, keepdims=True))
            share = 1.0 / jnp.sum(raised, -1, keepdims=True)
            total = jnp.where(mask, dot(raised.astype(BF16), v_out[...], 1, 0) * share, total)
        context[low:high] = total.astype(BF16)
    send[...] = dot(context[HALVES[1]], weights[:, 768:], 1, 1).astype(BF16)
    mine[...] = dot(context[HALVES[0]], weights[:, 768:], 1, 1)


def attend_forward(own, other, weights, bias, qv_bias):
    wide, half = (ROWS, 256), (HALF, D)
    return call(
        attend_forward_kernel,
        [(wide, BF16)] * 4 + [(half, BF16), (half, F32)],
        (own, other, weights, bias, qv_bias),
        "attend_forward",
    )


def attend_backward_kernel(
    own, other, weights, bias, q_in, k_in, v_in, grad_qk, grad_v, sums, ends, send, mine, keep, turned, tall
):
    for rows, part in zip(HALVES, (own, other)):
        keep[rows] = dot(part[...], weights[:, 768:], 1, 0).astype(BF16)
    turned[...] = jnp.zeros_like(turned)
    tall[ROWS:] = jnp.zeros((640 - ROWS, 256), F32)
    for head in range(4):
        mask = head_mask(head)
        tall[:ROWS] = jnp.where(mask, k_in[...].astype(F32) * 0.125, 0.0)
        keys = tall[:ROWS].astype(BF16)
        flat_keys = tall[...].T[:, :ROWS].astype(BF16)
        values = jnp.where(mask, v_in[...], 0.0).astype(BF16)
        total_k = jnp.zeros((ROWS, 256), F32)
        total_v = jnp.zeros((ROWS, 256), F32)
        for low, high in GRAD_CUTS:
            queries = q_in[low:high]
            scores = dot(keys, queries, 1, 1) + bias[...]
            raised = jnp.exp(scores - jnp.max(scores, 0, keepdims=True))
            probs = raised * (1.0 / jnp.sum(raised, 0, keepdims=True))
            grads = dot(values, keep[low:high], 1, 1)
            inner = jnp.sum(probs * grads, 0, keepdims=True)
            grad_scores = (probs * (grads - inner)).astype(BF16)
            total_k += dot(grad_scores, queries, 1, 0)
            total_v += dot(probs.astype(BF16), keep[low:high], 1, 0)
            turned[:, low:high] += dot(flat_keys, grad_scores, 1, 0)
        columns = slice(256, 512)
        if head:
            total_k = jnp.where(mask, total_k * 0.125, grad_qk[:, columns].astype(F32))
            total_v = jnp.where(mask, total_v, grad_v[...].astype(F32))
        else:
            total_k = total_k * 0.125
        grad_qk[:, columns] = total_k.astype(BF16)
        grad_v[...] = total_v.astype(BF16)
    grad_qk[:, :256] = turned[...].T[:ROWS].astype(BF16)
    sums[:, :256] = jnp.sum(grad_qk[:, :256].astype(F32), 0, keepdims=True)
    sums[:, 256:] = jnp.sum(grad_v[...].astype(F32), 0, keepdims=True)
    ends[...] = column_sums(own, other)
    for rows, out in zip(HALVES, (mine, send)):
        value = dot(grad_qk[rows], weights[:, :512], 1, 1)
        value += dot(grad_v[rows], weights[:, 512:768], 1, 1)
        out[...] = value.astype(out.dtype)


def attend_backward(own, other, weights, bias, queries, keys, values):
    half = (HALF, D)
    return call(
        attend_backward_kernel,
        [((ROWS, 512), BF16), ((ROWS, 256), BF16), ((1, 512), F32), ((1, D), F32)]
        + [(half, BF16), (half, F32)],
        (own, other, weights, bias, queries, keys, values),
        "attend_backward",
        scratch=(
            pltpu.VMEM((ROWS, 256), BF16),
            pltpu.VMEM((256, 640), F32),
            pltpu.VMEM((640, 256), F32),
        ),
    )


def mlp_forward_kernel(own, other, up, down, up_bias, active, slope, send, mine):
    for rows, part in zip(HALVES, (own, other)):
        for low in range(0, D, 256):
            columns = slice(low, low + 256)
            hidden = dot(part[...], up[:, columns], 1, 0) + up_bias[:, columns]
            share = 0.5 * (1.0 + lax.erf(hidden * 0.7071067811865476))
            density = 0.3989422804014327 * jnp.exp(-0.5 * hidden * hidden)
            active[rows, columns] = (hidden * share).astype(BF16)
            slope[rows, columns] = (share + hidden * density).astype(BF16)
    send[...] = dot(active[HALVES[1]], down[...], 1, 1).astype(BF16)
    mine[...] = dot(active[HALVES[0]], down[...], 1, 1)


def mlp_forward(own, other, up, down, up_bias):
    whole, half = (ROWS, D), (HALF, D)
    return call(
        mlp_forward_kernel,
        [(whole, BF16), (whole, BF16), (half, BF16), (half, F32)],
        (own, other, up, down, up_bias),
        "mlp_forward",
    )


def mlp_backward_kernel(own, other, up, down, slope, grad_hidden, sums, ends, send, mine):
    for rows, part in zip(HALVES, (own, other)):
        for low in range(0, D, 256):
            columns = slice(low, low + 256)
            value = dot(part[...], down[:, columns], 1, 0) * slope[rows, columns].astype(F32)
            grad_hidden[rows, columns] = value.astype(BF16)
    send[...] = dot(grad_hidden[HALVES[1]], up[...], 1, 1).astype(BF16)
    mine[...] = dot(grad_hidden[HALVES[0]], up[...], 1, 1)
    sums[...] = jnp.sum(grad_hidden[...].astype(F32), 0, keepdims=True)
    ends[...] = column_sums(own, other)


def mlp_backward(own, other, up, down, slope):
    whole, half = (ROWS, D), (HALF, D)
    return call(
        mlp_backward_kernel,
        [(whole, BF16), ((1, D), F32), ((1, D), F32), (half, BF16), (half, F32)],
        (own, other, up, down, slope),
        "mlp_backward",
    )


def feature_pairs(value, other, place):
    low = jnp.where(place.y == 0, value, other)
    high = jnp.where(place.y == 0, other, value)
    pair = jnp.concatenate([low, high], 1)
    return pair, swap(pair, "col", 1)


def gather_features(value, other, place):
    pair, arrived = feature_pairs(value, other, place)
    even = jnp.where(place.core == 0, pair, arrived)
    odd = jnp.where(place.core == 0, arrived, pair)
    return jnp.concatenate([even[:, :256], odd[:, :256], even[:, 256:], odd[:, 256:]], 1)


def whole_rows(pair, arrived, rows):
    core = lax.rem(lax.axis_index("col"), 2) == 0
    mine, other = pair[rows], arrived[rows]
    even, odd = jnp.where(core, mine, other), jnp.where(core, other, mine)
    return jnp.concatenate([even[:, :256], odd[:, :256], even[:, 256:], odd[:, 256:]], 1)


def halves_of(pair, arrived):
    core = lax.rem(lax.axis_index("col"), 2) == 0
    first = whole_rows(pair, arrived, slice(0, HALF))
    second = whole_rows(pair, arrived, slice(HALF, TOKENS))
    second = jnp.concatenate([second, jnp.zeros((ROWS - TOKENS, D), BF16)], 0)
    return jnp.where(core, first, second), jnp.where(core, second, first)


def order_kernel(pair, arrived, own, other):
    own[...], other[...] = halves_of(pair, arrived)


def order_halves(pair, arrived):
    return call(order_kernel, [((HALF, D), BF16)] * 2, (pair, arrived), "order_halves")


def enter_kernel(pair, arrived, gain, shift, resid, own, other):
    for out, value in zip((own, other), halves_of(pair, arrived)):
        value = value.astype(F32)
        if out is own:
            resid[...] = value
        out[...] = (norm(value)[0] * gain[...] + shift[...]).astype(BF16)


def enter(pair, arrived, gain, shift):
    half = (HALF, D)
    outs = [(half, F32), (half, BF16), (half, BF16)]
    return call(enter_kernel, outs, (pair, arrived, gain, shift), "enter")


def pick_kernel(own, kept, sent):
    col = lax.axis_index("col")
    for out, block in ((kept, col), (sent, col ^ 1)):
        out[...] = own[:, pl.ds(pl.multiple_of(block * 256, 256), 256)]


def merge_kernel(kept, arrived, out):
    core = lax.rem(lax.axis_index("col"), 2) == 0
    mine, other = kept[...], arrived[...]
    out[:HALF] = jnp.where(core, mine, other)
    out[HALF:] = jnp.where(core, other, mine)[: TOKENS - HALF]


def feature_block(own):
    part = ((HALF, 256), BF16)
    kept, sent = call(pick_kernel, [part, part], (own,), "pick_block")
    return call(
        merge_kernel, [((TOKENS, 256), BF16)], (kept, swap(sent, "col", 1)), "merge_block"
    )[0]


def small_kernel(sums, halves, arrived, *outs):
    col = lax.axis_index("col")
    columns = pl.ds(pl.multiple_of(col * 256, 256), 256)
    for index in range(6):
        value = (halves if index < 4 else sums)[index : index + 1, columns]
        if index < 2:
            value += arrived[index : index + 1, columns]
        outs[index][...] = value
    for index in range(2):
        outs[6][:, index] = sums[6:7, 256 * index : 256 * index + 256]
    outs[7][...] = sums[7:8]


def chip_sum(send, mine):
    return (mine + swap(send, "col", 1).astype(F32)).astype(BF16)


def col_sum(chip, arrived):
    return chip.astype(F32) + arrived.astype(F32)


def norm(resid):
    center = jnp.mean(resid, -1, keepdims=True)
    scale = lax.rsqrt(jnp.mean(resid * resid, -1, keepdims=True) - center * center + EPS)
    return (resid - center) * scale, scale


def norm_backward_kernel(chip, arrived, resid, gain, grad_out, *outs):
    grad = chip[...].astype(F32) + arrived[...].astype(F32)
    normal, scale = norm(resid[...])
    scaled = grad * gain[...]
    mean_one = jnp.mean(scaled, -1, keepdims=True)
    mean_two = jnp.mean(scaled * normal, -1, keepdims=True)
    total = grad_out[...].astype(F32) + scale * (scaled - mean_one - normal * mean_two)
    outs[0][...] = total.astype(BF16)
    if len(outs) > 1:
        outs[1][0:1] = jnp.sum(grad * normal, 0, keepdims=True)
        outs[1][1:2] = jnp.sum(grad, 0, keepdims=True)
        outs[2][...] = total


def norm_backward(chip, arrived, resid, gain, grad_out, wide):
    half = (HALF, D)
    outs = [(half, BF16)] + [((2, D), F32), (half, F32)] * wide
    return call(norm_backward_kernel, outs, (chip, arrived, resid, gain, grad_out), "norm_backward")


def norm_sums_kernel(chip, resid, sums):
    grad = chip[...].astype(F32)
    sums[0:1] = jnp.sum(grad * norm(resid[...])[0], 0, keepdims=True)
    sums[1:2] = jnp.sum(grad, 0, keepdims=True)


def norm_sums(chip, resid):
    return call(norm_sums_kernel, [((2, D), F32)], (chip, resid), "norm_sums")[0]


def pack_sums_kernel(*refs):
    *ins, out = refs
    for layer in range(2):
        one, two, qv, hidden, attend, mlp = ins[6 * layer : 6 * layer + 6]
        row = 8 * layer
        out[row : row + 2] = one[...]
        out[row + 2 : row + 4] = two[...]
        out[row + 4 : row + 5] = attend[...]
        out[row + 5 : row + 6] = mlp[...]
        out[row + 6 : row + 7, :512] = qv[...]
        out[row + 6 : row + 7, 512:] = jnp.zeros((1, 512), F32)
        out[row + 7 : row + 8] = hidden[...]


def mlp_part(ends, saved, weights):
    _, up, down = weights
    resid, one, qkv, context, middle, two, active, slope = saved
    grad_hidden, hidden_sum, mlp_sum, send, mine = mlp_backward(*ends, up, down, slope)
    chip = chip_sum(send, mine)
    pinned = lax.optimization_barrier((*two, *ends, grad_hidden, active, chip))
    two, ends, (grad_hidden, active) = pinned[0:2], pinned[2:4], pinned[4:6]
    return chip, swap(chip, "col", 2), (two, ends, grad_hidden, active), hidden_sum, mlp_sum


def attend_part(pair, saved, weights, bias, marks=()):
    resid, one, qkv, context, middle, two, active, slope = saved
    tall_bias = bias.reshape(ROWS, 1)
    grad_qk, grad_v, qv_sum, attend_sum, send, mine = attend_backward(
        *pair, weights[0], tall_bias, *qkv
    )
    chip = chip_sum(after(send, *marks) if marks else send, mine)
    pinned = lax.optimization_barrier((*one, *pair, grad_qk, grad_v, context, chip))
    one, pair, (grad_qk, grad_v, context) = pinned[0:2], pinned[2:4], pinned[4:7]
    parts = [(one, grad_qk)], [(one, grad_v), (pair, context)]
    return chip, swap(chip, "col", 2), parts, qv_sum, attend_sum


def local(
    layer_input,
    cotangent,
    norm1_gain,
    norm1_shift,
    qkv_weight,
    qv_bias,
    out_weight,
    out_bias,
    norm2_gain,
    norm2_shift,
    up_weight,
    up_bias,
    down_weight,
    down_bias,
):
    place = Place()
    leading = place.section == 0

    vectors = call(
        pack_kernel,
        [((16, 256), BF16)],
        (norm1_gain, norm1_shift, norm2_gain, norm2_shift, out_bias, down_bias, qv_bias, up_bias),
        "pack_vectors",
    )[0]
    narrow = [qkv_weight[0, :, 0], qkv_weight[0, :, 1], qkv_weight[0, :, 2], out_weight[0].T]
    attend_mine = jnp.concatenate(narrow, 1)
    mlp_mine = jnp.concatenate([up_weight[0], down_weight[0].T], 1)
    attend_other = swap(attend_mine, "section", 1)
    entry = layer_input[0, 0]
    entry_other = swap(entry, "col", 2)
    vectors_other = swap(vectors, "section", 1)
    mlp_other = swap(after(mlp_mine, attend_mine), "section", 1)
    attend = (
        jnp.where(leading, attend_mine, attend_other),
        jnp.where(leading, attend_other, attend_mine),
    )
    attend0 = gather_light(attend[0], "x")
    entry, entry_other, vectors, vectors_other, mlp_mine, mlp_other, _ = lax.optimization_barrier(
        (entry, entry_other, vectors, vectors_other, mlp_mine, mlp_other, attend0)
    )
    attend0 = Heavy(attend0, "x")
    marks = (attend0.near, attend0.far)
    attend0 = attend0.finish()

    vectors = (
        jnp.where(leading, vectors, vectors_other),
        jnp.where(leading, vectors_other, vectors),
    )
    both = jnp.concatenate(vectors, 0)
    both = gather_features(both, swap(both, "col", 2), place).astype(F32)
    params = []
    for layer in range(2):
        wide = tuple(both[16 * layer + i][None] for i in range(6))
        narrow = vectors[layer].astype(F32)
        params.append(wide + (narrow[6:8].reshape(1, 512), narrow[8:12].reshape(1, 1024)))
    entry = feature_pairs(entry, entry_other, place)

    mlp = (
        jnp.where(leading, mlp_mine, mlp_other),
        jnp.where(leading, mlp_other, mlp_mine),
    )
    up0 = gather_light(mlp[0][:, :1024], "x", *marks)
    down0 = gather_light(mlp[0][:, 1024:], "z", *marks)
    exit_grad = after(cotangent[0, 0], *marks)
    exit_other = swap(exit_grad, "col", 2)

    position = lax.broadcasted_iota(jnp.int32, (1, ROWS), 1)
    valid = TOKENS - HALF
    padding = jnp.where(
        place.core == 0, position >= TOKENS, jnp.logical_and(position >= valid, position < HALF)
    )
    bias = jnp.where(padding, -1e30, 0.0).astype(F32)

    gain1, shift1, gain2, shift2, out_bias0, down_bias0, qv_bias0, up_bias0 = params[0]
    resid0, *one0 = enter(*entry, gain1, shift1)
    one0 = lax.optimization_barrier((*one0, up0, down0, exit_other))[:2]
    up_steps = Heavy(after(up0, attend0), "x")
    down_steps = Heavy(down0, "z")
    *qkv0, context0, send, mine = attend_forward(*one0, attend0, bias, qv_bias0)
    send = after(send, up_steps.near, up_steps.far, down_steps.near, down_steps.far)
    chip = chip_sum(send, mine)
    up0 = up_steps.finish(chip)
    down0 = down_steps.finish(chip)
    attend1 = gather_light(after(attend[1], chip), "x")
    attend_steps = Heavy(after(attend1, up_steps.low, up_steps.high), "x")
    arrived = after(swap(chip, "col", 2), up0, down0, attend1)
    middle0 = resid0 + col_sum(chip, arrived) + out_bias0
    normal, _ = norm(middle0)
    two_own = (normal * gain2 + shift2).astype(BF16)
    two0 = (two_own, swap(two_own, "col", 1))
    active0, slope0, send, mine = mlp_forward(*two0, up0, down0, up_bias0)
    chip = chip_sum(after(send, attend_steps.near, attend_steps.far), mine)
    attend1 = attend_steps.finish(chip)
    marks = (attend_steps.low, attend_steps.high)
    up1 = gather_light(after(mlp[1][:, :1024], send), "x", *marks)
    down1 = gather_light(after(mlp[1][:, 1024:], send), "z", *marks)
    arrived = after(swap(chip, "col", 2), attend1, up1, down1)
    section_mid = (middle0 + col_sum(chip, arrived) + down_bias0).astype(BF16)

    gain1, shift1, gain2, shift2, out_bias1, down_bias1, qv_bias1, up_bias1 = params[1]
    resid1 = section_mid.astype(F32)
    normal, _ = norm(resid1)
    one_own = (normal * gain1 + shift1).astype(BF16)
    one_own = after(one_own, up1, down1)
    one1 = (one_own, swap(one_own, "col", 1))
    up_steps = Heavy(after(up1, attend1), "x")
    down_steps = Heavy(down1, "z")
    *qkv1, context1, send, mine = attend_forward(*one1, attend1, bias, qv_bias1)
    send = after(send, up_steps.near, up_steps.far, down_steps.near, down_steps.far)
    chip = chip_sum(send, mine)
    up1 = up_steps.finish(chip)
    down1 = down_steps.finish(chip)
    ends = order_halves(*feature_pairs(exit_grad, exit_other, place))
    arrived = after(swap(chip, "col", 2), *ends, up1, down1)
    middle1 = resid1 + col_sum(chip, arrived) + out_bias1
    normal, _ = norm(middle1)
    two_own = (normal * gain2 + shift2).astype(BF16)
    two1 = (two_own, swap(two_own, "col", 1))
    active1, slope1, final_send, final_mine = mlp_forward(*two1, up1, down1, up_bias1)

    gains = (params[0][0], params[0][2], params[1][0], params[1][2])
    weights = (attend1, up1, down1)
    saved = (resid1, one1, qkv1, context1, middle1, two1, active1, slope1)
    chip, arrived, parts, hidden_sum1, mlp_sum1 = mlp_part(ends, saved, weights)
    two, ends, grad_hidden, active = parts
    grads = weight_grads([(two, grad_hidden)], [(ends, active)], "mlp_grad")
    second_ring_x, second_ring_z = Ring("x", *grads[:5]), Ring("z", *grads[5:])
    final_send, final_mine, _ = lax.optimization_barrier((final_send, final_mine, chip))
    final_chip = chip_sum(final_send, final_mine)
    marks = (second_ring_x.low, second_ring_x.high, second_ring_z.low, second_ring_z.high)
    arrived = after(arrived, *grads, final_chip, *marks)
    own, two_sums1, grad_middle = norm_backward(chip, arrived, middle1, gains[3], ends[0], True)
    pair = (own, swap(own, "col", 1))

    chip, arrived, parts, qv_sum1, attend_sum1 = attend_part(pair, saved, weights, bias)
    attend_blocks = weight_grads(*parts, "attend_grad")
    second_x, second_z = second_ring_x.finish(chip), second_ring_z.finish(chip)
    one_sums1 = norm_sums(chip, resid1)
    arrived = after(
        arrived, *attend_blocks, one_sums1, *second_ring_x.sent, *second_ring_z.sent
    )
    grad_mid = norm_backward(chip, arrived, resid1, gains[2], grad_middle, False)[0]

    ends = (grad_mid, swap(grad_mid, "col", 1))
    weights = (attend0, up0, down0)
    saved = (resid0, one0, qkv0, context0, middle0, two0, active0, slope0)
    chip, arrived, parts, hidden_sum0, mlp_sum0 = mlp_part(ends, saved, weights)
    two, ends, grad_hidden, active = parts
    grads = weight_grads([(two, grad_hidden)], [(ends, active)], "mlp_grad", attend_blocks)
    ring_x, ring_z = Ring("x", *grads[:5]), Ring("z", *grads[5:])
    arrived = after(arrived, *grads, *second_x, *second_z)
    own, two_sums0, grad_middle = norm_backward(chip, arrived, middle0, gains[1], ends[0], True)
    pair = (own, swap(own, "col", 1))
    marks = (ring_x.low, ring_x.high, ring_z.low, ring_z.high)
    chip, arrived, parts, qv_sum0, attend_sum0 = attend_part(pair, saved, weights, bias, marks)
    sums = (norm_sums(chip, resid0), two_sums0, qv_sum0, hidden_sum0, attend_sum0, mlp_sum0)
    sums += (one_sums1, two_sums1, qv_sum1, hidden_sum1, attend_sum1, mlp_sum1)
    sums = call(pack_sums_kernel, [((16, D), F32)], sums, "pack_sums")
    grads = weight_grads(*parts, "attend_grad", ride=sums)
    attend_ring_x, attend_ring_z = Ring("x", *grads[:5]), Ring("z", *grads[5:])
    marks = (attend_ring_x.low, attend_ring_x.high, attend_ring_z.low, attend_ring_z.high)
    parts_x = ring_x.finish(*marks, beside=(attend_ring_x,), ride=sums)
    parts_z = ring_z.finish(*marks, beside=(attend_ring_z,))
    arrived = after(arrived, *ring_x.sent, *ring_z.sent)
    input_own = norm_backward(chip, arrived, resid0, gains[0], grad_middle, False)[0]

    input_grad = feature_block(input_own)
    parts_x = lax.optimization_barrier((*parts_x, input_grad))[:3]
    parts_z = lax.optimization_barrier((*parts_z, input_grad))[:3]
    light_x = light_ring("x", parts_x, second_x, ride=ring_x.ride)
    light_z = light_ring("z", parts_z, second_z)
    marks = (light_x.low, light_x.high, light_z.low, light_z.high)
    total_x, sums = light_sum(light_x, *marks)
    total_z = light_sum(light_z, *marks)

    final_chip = after(final_chip, *ring_x.sent, *ring_z.sent)
    final_arrived = swap(final_chip, "col", 2)
    final_chip = after(final_chip, total_z)
    final = middle1 + col_sum(final_chip, final_arrived) + down_bias1
    final = feature_block(final.astype(BF16))
    total_x = after(total_x, final)
    def for_sections(first, second):
        sent = jnp.where(leading, second, first).astype(BF16)
        return jnp.where(leading, first, second), sent

    mine, sent = for_sections(
        jnp.concatenate([total_x[:, :1024], total_z[:, :1024]], 1),
        jnp.concatenate([total_x[:, 2048:], total_z[:, 2048:]], 1),
    )
    total_mlp = mine + swap(sent, "section", 1).astype(F32)
    mine, sent = for_sections(
        jnp.concatenate([total_x[:, 1536:2048], total_z[:, 1536:2048]], 1),
        jnp.concatenate([total_x[:, 1024:1536], total_z[:, 1024:1536]], 1),
    )
    sums, sums_sent = for_sections(sums[:8], sums[8:])
    arrived = swap(jnp.concatenate([sent, sums_sent, sums_sent], 0), "section", 1).astype(F32)
    total_attend = mine + arrived[:64]
    sums = sums + arrived[64:72]
    total_qkv = total_attend[:, :768].reshape(64, 3, 256)
    total_vo = total_attend[:, 768:]
    total_up, total_down = total_mlp[:, :1024], total_mlp[:, 1024:]

    outs = [((1, 256), F32)] * 6 + [((1, 2, 256), F32), ((1, 1024), F32)]
    halves = sums[:4] + swap(sums[:4], "col", 1)
    small = call(small_kernel, outs, (sums, halves, swap(halves[:2], "col", 2)), "small_outputs")

    return (
        final[None, None],
        input_grad[None, None],
        small[0],
        small[1],
        total_qkv[None],
        small[6],
        total_vo.T[None],
        small[4],
        small[2],
        small[3],
        total_up[None],
        small[7],
        total_down.T[None],
        small[5],
    )


def solution(mesh):
    placed = (
        P("section", "row", None, "col"),
        P("section", "row", None, "col"),
        P("section", "col"),
        P("section", "col"),
        P("section", "row", None, "col"),
        P("section", None, "col"),
        P("section", "col", "row"),
        P("section", "col"),
        P("section", "col"),
        P("section", "col"),
        P("section", "row", "col"),
        P("section", "col"),
        P("section", "col", "row"),
        P("section", "col"),
    )
    return jax.shard_map(
        local,
        mesh=mesh,
        in_specs=placed,
        out_specs=placed,
        check_vma=False,
    )
```

time: 1310 us -> 363 us (0.28)
  waiting for transfers between devices: 827 us -> 150 us
  matrix products: 182 us -> 0 us
  blocking collectives: 163 us -> 0 us
  starting transfers between devices: 13.2 us -> 127 us
  Pallas kernels: 0 us -> 66.1 us
  other arithmetic: 53.3 us -> 7.61 us
  local copies, waits for them, and re-layouts: 43 us -> 3.6 us
  between operations: 16.7 us -> 1.94 us
    reduce_scatter x15 -> x0, waiting for transfers between devices: 406 us -> none  [the longest x6 130 us: input_sum(): lax.psum_scatter(partial_sum.astype(jnp.bfloat16), 'col', scatter_dimensi...]
    all_gather x15 -> x0, waiting for transfers between devices: 354 us -> none  [the longest x6 121 us: norm_forward(): lax.all_gather((normal * gain + shift).astype(jnp.bfloat16), 'col', axis=...]
    dot_general x54 -> x0, matrix products: 182 us -> none  [the longest x3 28.5 us: layer_forward(): jnp.einsum('isd,df->isf', features_two, up_full, preferred_element_type=j...]
    psum x13 -> x0, blocking collectives: 142 us -> none  [the longest x1 60.8 us: local(): summed = lax.psum(small_total, 'row')]
    ppermute x4 -> x107, waiting for transfers between devices: 28.5 us -> 150 us  [swap(): lax.ppermute(value, axis, [(i, i ^ mask) for i in range(lax.axis_size(axi...]
    ppermute x4 -> x107, starting transfers between devices: 9.84 us -> 127 us  [swap(): lax.ppermute(value, axis, [(i, i ^ mask) for i in range(lax.axis_size(axi...]
    pallas_call x0 -> x47, Pallas kernels: none -> 66.1 us  [call(): pl.pallas_call(kernel, out_shape=[jax.ShapeDtypeStruct(*out) for out in o...]
    unnamed x32 -> x0, waiting for transfers between devices: 38.6 us -> none
  transfers between devices with their start and end apart: 35 -> 107, of which waited for: 33 -> 59; matrix products, arithmetic and copies ran while one was open for 8% -> 1% of each run, Pallas kernels for 0% -> 11%
where the time goes in v1:
time: 363 us; the launch traced here: 357 us
  waiting for transfers between devices  150 us (41%)
  starting transfers between devices  127 us (35%)
  Pallas kernels  66.1 us (18%)
  other arithmetic  7.61 us (2%)
    ppermute x107, waiting for transfers between devices, swap(): lax.ppermute(value, axis, [(i, i ^ mask) for i in range(lax.axis_size(axi...  150 us
    ppermute x107, starting transfers between devices, swap(): lax.ppermute(value, axis, [(i, i ^ mask) for i in range(lax.axis_size(axi...  127 us
    pallas_call x47, Pallas kernels, call(): pl.pallas_call(kernel, out_shape=[jax.ShapeDtypeStruct(*out) for out in o...  66.1 us
  transfers between devices with their start and end apart: 107, of which 59 were waited for; matrix products, arithmetic and copies ran while one was open for 1% of the time, Pallas kernels for 11%

profile of v1, /device:TPU:1, one launch (start us, length us, event | category | flops | bytes accessed | tf_op | source)
XLA Modules:
  0.0 356.7 jit_solution(11606834749627817122)
XLA Ops:
  2.3 3.8 %collective-permute-start.3 = (bf16[64,1024]{1,0:T(8,128)(2,1)S(1)}, bf16[64,1024]{1,0:T(8,128)(2,1)S(1)}, u32[]{:S(2)}, u32[]{:S(2)}) collective-permute-start(bf16[64,1024]{1,0:T(8,128)(2,1)S(1)} %pad_maximum_fusion.8), channel_id=1, source_target_pairs={{0,64},{64,0},{1,65},{65,1},{2,66},{66,2},{3,67},{67,3},{4,68},{68... | collective-permute-start | bytes 393224 | tf_op jit(solution)/shard_map/ppermute | solution.py:22
  9.9 3.8 %collective-permute-start.4 = (bf16[64,1024]{1,0:T(8,128)(2,1)S(1)}, bf16[64,1024]{1,0:T(8,128)(2,1)S(1)}, u32[]{:S(2)}, u32[]{:S(2)}) collective-permute-start(bf16[64,1024]{1,0:T(8,128)(2,1)S(1)} %get-tuple-element.557.refs_0_), channel_id=1, source_target_pairs={{0,12},{4,8},{8,4},{12,0},{16,28},{20,24},{24,20},{28,16},{32,44},... | collective-permute-start | bytes 393224 | tf_op jit(solution)/shard_map/ppermute | solution.py:22
  14.8 3.0 collective-permute-start.2
  27.1 6.8 %collective-permute-done.12.near = bf16[256,1024]{1,0:T(8,128)(2,1)S(1)} collective-permute-done((bf16[256,1024]{1,0:T(8,128)(2,1)S(1)}, bf16[256,1024]{1,0:T(8,128)(2,1)S(1)}, u32[]{:S(2)}, u32[]{:S(2)}) %collective-permute-start.12) | collective-permute-done | bytes 524320 | tf_op jit(solution)/shard_map/ppermute | solution.py:22
  44.0 7.5 %collective-permute-start.9 = (bf16[32,512]{1,0:T(8,128)(2,1)S(1)}, bf16[32,512]{1,0:T(8,128)(2,1)S(1)}, u32[]{:S(2)}, u32[]{:S(2)}) collective-permute-start(bf16[32,512]{1,0:T(8,128)(2,1)S(1)} %pad_maximum_fusion.9), channel_id=1, source_target_pairs={{0,1},{1,0},{2,3},{3,2},{4,5},{5,4},{6,7},{7,6},{8,9},{9,8},{10,11... | collective-permute-start | bytes 98312 | tf_op jit(solution)/shard_map/ppermute | solution.py:22
  51.8 3.0 collective-permute-start.7
  59.4 4.0 %attend_forward.2 = (bf16[608,256]{1,0:T(8,128)(2,1)S(1)}, bf16[608,256]{1,0:T(8,128)(2,1)S(1)}, bf16[608,256]{1,0:T(8,128)(2,1)S(1)}, bf16[608,256]{1,0:T(8,128...) custom-call(bf16[304,1024]{1,0:T(8,128)(2,1)S(1)} %get-tuple-element.403.own.refs_0_.refs_3_, ...), custom_call_target="tpu_custom_call" | custom-call | tf_op jit(solution)/shard_map/attend_forward/pallas_call | solution.py:57
  63.4 6.8 %collective-permute-done.23.near = bf16[4,64,1024]{2,1,0:T(8,128)(2,1)S(1)} collective-permute-done((bf16[4,64,1024]{2,1,0:T(8,128)(2,1)S(1)}, bf16[4,64,1024]{2,1,0:T(8,128)(2,1)S(1)}, u32[]{:S(2)}, u32[]{:S(2)}) %collective-permute-start.23) | collective-permute-done | bytes 524320 | tf_op jit(solution)/shard_map/ppermute | solution.py:22
  89.0 3.2 collective-permute-done.33.refs_3_
  97.1 3.7 %mlp_forward.2 = (bf16[608,1024]{1,0:T(8,128)(2,1)S(1)}, bf16[608,1024]{1,0:T(8,128)(2,1)S(1)}, bf16[304,1024]{1,0:T(8,128)(2,1)S(1)}, f32[304,1024]{1,0:T(8,128)S(1)}) custom-call(bf16[304,1024]{1,0:T(8,128)(2,1)S(1)} %add_convert_fusion.11.own.refs_0_, bf16[304,1024]{1,0:T(8,128)(2,1)S(1)} %collective-permute-done.34.other.refs_1_, ...), custom_call_target="tpu_custom_call" | custom-call | tf_op jit(solution)/shard_map/mlp_forward/pallas_call | solution.py:57
  100.8 8.8 %collective-permute-done.35.near = bf16[256,1024]{1,0:T(8,128)(2,1)S(1)} collective-permute-done((bf16[256,1024]{1,0:T(8,128)(2,1)S(1)}, bf16[256,1024]{1,0:T(8,128)(2,1)S(1)}, u32[]{:S(2)}, u32[]{:S(2)}) %collective-permute-start.35) | collective-permute-done | bytes 524320 | tf_op jit(solution)/shard_map/ppermute | solution.py:22
  130.2 2.8 collective-permute-start.47
  136.1 4.0 %attend_forward.3 = (bf16[608,256]{1,0:T(8,128)(2,1)S(1)}, bf16[608,256]{1,0:T(8,128)(2,1)S(1)}, bf16[608,256]{1,0:T(8,128)(2,1)S(1)}, bf16[608,256]{1,0:T(8,128...) custom-call(bf16[304,1024]{1,0:T(8,128)(2,1)S(1)} %add_convert_fusion.8.own.refs_0_.refs_3_, ...), custom_call_target="tpu_custom_call" | custom-call | tf_op jit(solution)/shard_map/attend_forward/pallas_call | solution.py:57
  140.1 7.5 %collective-permute-done.48.near = bf16[256,1024]{1,0:T(8,128)(2,1)S(1)} collective-permute-done((bf16[256,1024]{1,0:T(8,128)(2,1)S(1)}, bf16[256,1024]{1,0:T(8,128)(2,1)S(1)}, u32[]{:S(2)}, u32[]{:S(2)}) %collective-permute-start.48) | collective-permute-done | bytes 524320 | tf_op jit(solution)/shard_map/ppermute | solution.py:22
  163.9 3.6 %collective-permute-done.53 = bf16[304,1024]{1,0:T(8,128)(2,1)S(1)} collective-permute-done((bf16[304,1024]{1,0:T(8,128)(2,1)S(1)}, bf16[304,1024]{1,0:T(8,128)(2,1)S(1)}, u32[]{:S(2)}, u32[]{:S(2)}) %collective-permute-start.53) | collective-permute-done | bytes 622624 | tf_op jit(solution)/shard_map/ppermute | solution.py:22
  171.7 3.7 %mlp_forward.3 = (bf16[608,1024]{1,0:T(8,128)(2,1)S(1)}, bf16[608,1024]{1,0:T(8,128)(2,1)S(1)}, bf16[304,1024]{1,0:T(8,128)(2,1)S(1)}, f32[304,1024]{1,0:T(8,128)S(1)}) custom-call(bf16[304,1024]{1,0:T(8,128)(2,1)S(1)} %add_convert_fusion.6.own.refs_0_, bf16[304,1024]{1,0:T(8,128)(2,1)S(1)} %collective-permute-done.59.other.refs_1_, ...), custom_call_target="tpu_custom_call" | custom-call | tf_op jit(solution)/shard_map/mlp_forward/pallas_call | solution.py:57
  175.4 3.1 mlp_backward.2
  181.5 4.0 %mlp_grad.2 = (bf16[256,1024]{1,0:T(8,128)(2,1)S(1)}, bf16[256,1024]{1,0:T(8,128)(2,1)S(1)}, bf16[256,1024]{1,0:T(8,128)(2,1)S(1)}, bf16[128,1024]{1,0:T(8,128)(...) custom-call(bf16[304,1024]{1,0:T(8,128)(2,1)S(1)} %add_convert_fusio, ...), custom_call_target="tpu_custom_call" | custom-call | tf_op jit(solution)/shard_map/mlp_grad/pallas_call | solution.py:57
  201.7 9.6 %attend_backward.2 = (bf16[608,512]{1,0:T(8,128)(2,1)S(1)}, bf16[608,256]{1,0:T(8,128)(2,1)S(1)}, f32[1,512]{1,0:T(1,128)S(1)}, f32[1,1024]{1,0:T(1,128)S(1)}, b...) custom-call(bf16[304,1024]{1,0:T(8,128)(2,1)S(1)} %get-tuple-element.344.own.refs_6_, ...), custom_call_target="tpu_custom_call" | custom-call | tf_op jit(solution)/shard_map/attend_backward/pallas_call | solution.py:57
  217.8 11.5 %collective-permute-done.69.arrived = bf16[304,1024]{1,0:T(8,128)(2,1)S(1)} collective-permute-done((bf16[304,1024]{1,0:T(8,128)(2,1)S(1)}, bf16[304,1024]{1,0:T(8,128)(2,1)S(1)}, u32[]{:S(2)}, u32[]{:S(2)}) %collective-permute-start.69) | collective-permute-done | bytes 622624 | tf_op jit(solution)/shard_map/ppermute | solution.py:22
  233.1 3.2 mlp_backward.3
  242.0 4.0 %mlp_grad.3 = (bf16[256,1536]{1,0:T(8,128)(2,1)S(1)}, bf16[256,1536]{1,0:T(8,128)(2,1)S(1)}, bf16[256,1536]{1,0:T(8,128)(2,1)S(1)}, bf16[128,1536]{1,0:T(8,128)(...) custom-call(bf16[304,1024]{1,0:T(8,128)(2,1)S(1)} %add_convert_fusio, ...), custom_call_target="tpu_custom_call" | custom-call | tf_op jit(solution)/shard_map/mlp_grad/pallas_call | solution.py:57
  246.0 7.5 %collective-permute-done.75.refs_4_ = bf16[4,64,1024]{2,1,0:T(8,128)(2,1)S(1)} collective-permute-done((bf16[4,64,1024]{2,1,0:T(8,128)(2,1)S(1)}, bf16[4,64,1024]{2,1,0:T(8,128)(2,1)S(1)}, u32[]{:S(2)}, u32[]{:S(2)}) %collective-permute-start.75) | collective-permute-done | bytes 524320 | tf_op jit(solution)/shard_map/ppermute | solution.py:22
  262.2 9.6 %attend_backward.3 = (bf16[608,512]{1,0:T(8,128)(2,1)S(1)}, bf16[608,256]{1,0:T(8,128)(2,1)S(1)}, f32[1,512]{1,0:T(1,128)S(1)}, f32[1,1024]{1,0:T(1,128)S(1)}, b...) custom-call(bf16[304,1024]{1,0:T(8,128)(2,1)S(1)} %get-tuple-element.407.own.refs_6_, ...), custom_call_target="tpu_custom_call" | custom-call | tf_op jit(solution)/shard_map/attend_backward/pallas_call | solution.py:57
  281.9 2.6 collective-permute-done.85.refs_8_
  290.1 12.3 %collective-permute-done.89.arrived = bf16[304,1024]{1,0:T(8,128)(2,1)S(1)} collective-permute-done((bf16[304,1024]{1,0:T(8,128)(2,1)S(1)}, bf16[304,1024]{1,0:T(8,128)(2,1)S(1)}, u32[]{:S(2)}, u32[]{:S(2)}) %collective-permute-start.89) | collective-permute-done | bytes 622624 | tf_op jit(solution)/shard_map/ppermute | solution.py:22
  303.3 3.6 collective-permute-start.90
  317.0 3.4 collective-permute-done.95.refs_3_
  325.7 4.3 %collective-permute-done.97 = bf16[64,3072]{1,0:T(8,128)(2,1)S(1)} collective-permute-done((bf16[64,3072]{1,0:T(8,128)(2,1)S(1)}, bf16[64,3072]{1,0:T(8,128)(2,1)S(1)}, u32[]{:S(2)}, u32[]{:S(2)}) %collective-permute-start.97) | collective-permute-done | bytes 393248 | tf_op jit(solution)/shard_map/ppermute | solution.py:22
  330.2 2.7 collective-permute-done.99
  333.3 6.8 %collective-permute-start.100 = (bf16[304,256]{1,0:T(8,128)(2,1)S(1)}, bf16[304,256]{1,0:T(8,128)(2,1)S(1)}, u32[]{:S(2)}, u32[]{:S(2)}) collective-permute-start(bf16[304,256]{1,0:T(8,128)(2,1)S(1)} %get-tuple-element.475), channel_id=1, source_target_pairs={{0,1},{1,0},{2,3},{3,2},{4,5},{5,4},{6,7},{7,6},{8,9},{9,8},{10,11... | collective-permute-start | bytes 466952 | tf_op jit(solution)/shard_map/ppermute | solution.py:22
  345.2 3.8 %collective-permute-done.103 = bf16[80,1024]{1,0:T(8,128)(2,1)S(1)} collective-permute-done((bf16[80,1024]{1,0:T(8,128)(2,1)S(1)}, bf16[80,1024]{1,0:T(8,128)(2,1)S(1)}, u32[]{:S(2)}, u32[]{:S(2)}) %collective-permute-start.103) | collective-permute-done | bytes 163872 | tf_op jit(solution)/shard_map/ppermute | solution.py:22
  (330 shorter events, 186.5 us)
Async XLA Ops:
  6.2 19.7 %collective-permute-start = (bf16[577,256]{1,0:T(8,128)(2,1)}, bf16[577,256]{1,0:T(8,128)(2,1)S(1)}, u32[]{:S(2)}, u32[]{:S(2)}) collective-permute-start(bf16[577,256]{1,0:T(8,128)(2,1)} %bitcast.98), channel_id=1, source_target_pairs={{0,2},{1,3},{2,0},{3,1},{4,6},{5,7},{6,4},{7,5},{8,10},{9,11},{10,... | collective-permute-start | bytes 886280 | tf_op jit(solution)/shard_map/ppermute | solution.py:22
  27.1 16.8 %collective-permute-start.11 = (bf16[64,1024]{1,0:T(8,128)(2,1)S(1)}, bf16[64,1024]{1,0:T(8,128)(2,1)S(1)}, u32[]{:S(2)}, u32[]{:S(2)}) collective-permute-start(bf16[64,1024]{1,0:T(8,128)(2,1)S(1)} %get-tuple-element.559.refs_0_), channel_id=1, source_target_pairs={{0,4},{4,0},{8,12},{12,8},{16,20},{20,16},{24,28},{28,24},{32,36},... | collective-permute-start | bytes 393224 | tf_op jit(solution)/shard_map/ppermute | solution.py:22
  36.4 15.0 %collective-permute-start.16 = (bf16[64,1024]{1,0:T(8,128)(2,1)S(1)}, bf16[64,1024]{1,0:T(8,128)(2,1)S(1)}, u32[]{:S(2)}, u32[]{:S(2)}) collective-permute-start(bf16[64,1024]{1,0:T(8,128)(2,1)S(1)} %get-tuple-element.558.refs_0_), channel_id=1, source_target_pairs={{0,16},{4,20},{8,24},{12,28},{16,0},{20,4},{24,8},{28,12},{32,48},... | collective-permute-start | bytes 393224 | tf_op jit(solution)/shard_map/ppermute | solution.py:22
  36.6 19.9 %collective-permute-start.19 = (bf16[128,1024]{1,0:T(8,128)(2,1)S(1)}, bf16[128,1024]{1,0:T(8,128)(2,1)S(1)}, u32[]{:S(2)}, u32[]{:S(2)}) collective-permute-start(bf16[128,1024]{1,0:T(8,128)(2,1)S(1)} %slice.189), channel_id=1, source_target_pairs={{0,16},{4,20},{8,24},{12,28},{16,0},{20,4},{24,8},{28,12},{32,48},... | collective-permute-start | bytes 786440 | tf_op jit(solution)/shard_map/ppermute | solution.py:22
  39.7 17.3 %collective-permute-start.20 = (bf16[128,1024]{1,0:T(8,128)(2,1)S(1)}, bf16[128,1024]{1,0:T(8,128)(2,1)S(1)}, u32[]{:S(2)}, u32[]{:S(2)}) collective-permute-start(bf16[128,1024]{1,0:T(8,128)(2,1)S(1)} %slice.190), channel_id=1, source_target_pairs={{0,48},{4,52},{8,56},{12,60},{16,32},{20,36},{24,40},{28,44},{32,1... | collective-permute-start | bytes 786440 | tf_op jit(solution)/shard_map/ppermute | solution.py:22
  44.0 13.5 %collective-permute-start.9 = (bf16[32,512]{1,0:T(8,128)(2,1)S(1)}, bf16[32,512]{1,0:T(8,128)(2,1)S(1)}, u32[]{:S(2)}, u32[]{:S(2)}) collective-permute-start(bf16[32,512]{1,0:T(8,128)(2,1)S(1)} %pad_maximum_fusion.9), channel_id=1, source_target_pairs={{0,1},{1,0},{2,3},{3,2},{4,5},{5,4},{6,7},{7,6},{8,9},{9,8},{10,11... | collective-permute-start | bytes 98312 | tf_op jit(solution)/shard_map/ppermute | solution.py:22
  56.5 13.8 %collective-permute-start.23 = (bf16[4,64,1024]{2,1,0:T(8,128)(2,1)S(1)}, bf16[4,64,1024]{2,1,0:T(8,128)(2,1)S(1)}, u32[]{:S(2)}, u32[]{:S(2)}) collective-permute-start(bf16[4,64,1024]{2,1,0:T(8,128)(2,1)S(1)} %place_blocks.14.own), channel_id=1, source_target_pairs={{0,12},{4,8},{8,4},{12,0},{16,28},{20,24},{24,20},{28,16},{32,44},... | collective-permute-start | bytes 1572872 | tf_op jit(solution)/shard_map/ppermute | solution.py:22
  56.5 13.7 %collective-permute-start.24 = (bf16[4,64,1024]{2,1,0:T(8,128)(2,1)S(1)}, bf16[4,64,1024]{2,1,0:T(8,128)(2,1)S(1)}, u32[]{:S(2)}, u32[]{:S(2)}) collective-permute-start(bf16[4,64,1024]{2,1,0:T(8,128)(2,1)S(1)} %place_blocks.14.own), channel_id=1, source_target_pairs={{0,4},{4,0},{8,12},{12,8},{16,20},{20,16},{24,28},{28,24},{32,36},... | collective-permute-start | bytes 1572872 | tf_op jit(solution)/shard_map/ppermute | solution.py:22
  57.1 13.6 %collective-permute-start.21 = (bf16[256,1024]{1,0:T(8,128)(2,1)S(1)}, bf16[256,1024]{1,0:T(8,128)(2,1)S(1)}, u32[]{:S(2)}, u32[]{:S(2)}) collective-permute-start(bf16[256,1024]{1,0:T(8,128)(2,1)S(1)} %bitcast.81), channel_id=1, source_target_pairs={{0,48},{4,52},{8,56},{12,60},{16,32},{20,36},{24,40},{28,44},{32,1... | collective-permute-start | bytes 1572872 | tf_op jit(solution)/shard_map/ppermute | solution.py:22
  57.4 13.3 %collective-permute-start.22 = (bf16[256,1024]{1,0:T(8,128)(2,1)S(1)}, bf16[256,1024]{1,0:T(8,128)(2,1)S(1)}, u32[]{:S(2)}, u32[]{:S(2)}) collective-permute-start(bf16[256,1024]{1,0:T(8,128)(2,1)S(1)} %bitcast.82), channel_id=1, source_target_pairs={{0,16},{4,20},{8,24},{12,28},{16,0},{20,4},{24,8},{28,12},{32,48},... | collective-permute-start | bytes 1572872 | tf_op jit(solution)/shard_map/ppermute | solution.py:22
  74.6 17.7 %collective-permute-start.26 = (bf16[304,1024]{1,0:T(8,128)(2,1)S(1)}, bf16[304,1024]{1,0:T(8,128)(2,1)S(1)}, u32[]{:S(2)}, u32[]{:S(2)}) collective-permute-start(bf16[304,1024]{1,0:T(8,128)(2,1)S(1)} %add_convert_fusion.12), channel_id=1, source_target_pairs={{0,2},{1,3},{2,0},{3,1},{4,6},{5,7},{6,4},{7,5},{8,10},{9,11},{10,... | collective-permute-start | bytes 1867784 | tf_op jit(solution)/shard_map/ppermute | solution.py:22
  94.9 14.7 %collective-permute-start.35 = (bf16[256,1024]{1,0:T(8,128)(2,1)S(1)}, bf16[256,1024]{1,0:T(8,128)(2,1)S(1)}, u32[]{:S(2)}, u32[]{:S(2)}) collective-permute-start(bf16[256,1024]{1,0:T(8,128)(2,1)S(1)} %bitcast.84), channel_id=1, source_target_pairs={{0,48},{4,52},{8,56},{12,60},{16,32},{20,36},{24,40},{28,44},{32,1... | collective-permute-start | bytes 1572872 | tf_op jit(solution)/shard_map/ppermute | solution.py:22
  96.9 13.3 %collective-permute-start.36 = (bf16[256,1024]{1,0:T(8,128)(2,1)S(1)}, bf16[256,1024]{1,0:T(8,128)(2,1)S(1)}, u32[]{:S(2)}, u32[]{:S(2)}) collective-permute-start(bf16[256,1024]{1,0:T(8,128)(2,1)S(1)} %bitcast.85), channel_id=1, source_target_pairs={{0,16},{4,20},{8,24},{12,28},{16,0},{20,4},{24,8},{28,12},{32,48},... | collective-permute-start | bytes 1572872 | tf_op jit(solution)/shard_map/ppermute | solution.py:22
  113.3 16.0 %collective-permute-start.38 = (bf16[304,1024]{1,0:T(8,128)(2,1)S(1)}, bf16[304,1024]{1,0:T(8,128)(2,1)S(1)}, u32[]{:S(2)}, u32[]{:S(2)}) collective-permute-start(bf16[304,1024]{1,0:T(8,128)(2,1)S(1)} %add_convert_fusion.10), channel_id=1, source_target_pairs={{0,2},{1,3},{2,0},{3,1},{4,6},{5,7},{6,4},{7,5},{8,10},{9,11},{10,... | collective-permute-start | bytes 1867784 | tf_op jit(solution)/shard_map/ppermute | solution.py:22
  133.0 14.7 %collective-permute-start.48 = (bf16[256,1024]{1,0:T(8,128)(2,1)S(1)}, bf16[256,1024]{1,0:T(8,128)(2,1)S(1)}, u32[]{:S(2)}, u32[]{:S(2)}) collective-permute-start(bf16[256,1024]{1,0:T(8,128)(2,1)S(1)} %bitcast.78), channel_id=1, source_target_pairs={{0,48},{4,52},{8,56},{12,60},{16,32},{20,36},{24,40},{28,44},{32,1... | collective-permute-start | bytes 1572872 | tf_op jit(solution)/shard_map/ppermute | solution.py:22
  134.1 13.6 %collective-permute-start.49 = (bf16[256,1024]{1,0:T(8,128)(2,1)S(1)}, bf16[256,1024]{1,0:T(8,128)(2,1)S(1)}, u32[]{:S(2)}, u32[]{:S(2)}) collective-permute-start(bf16[256,1024]{1,0:T(8,128)(2,1)S(1)} %bitcast.79), channel_id=1, source_target_pairs={{0,16},{4,20},{8,24},{12,28},{16,0},{20,4},{24,8},{28,12},{32,48},... | collective-permute-start | bytes 1572872 | tf_op jit(solution)/shard_map/ppermute | solution.py:22
  134.1 14.4 %collective-permute-start.50 = (bf16[4,64,1024]{2,1,0:T(8,128)(2,1)S(1)}, bf16[4,64,1024]{2,1,0:T(8,128)(2,1)S(1)}, u32[]{:S(2)}, u32[]{:S(2)}) collective-permute-start(bf16[4,64,1024]{2,1,0:T(8,128)(2,1)S(1)} %place_blocks.21.own), channel_id=1, source_target_pairs={{0,12},{4,8},{8,4},{12,0},{16,28},{20,24},{24,20},{28,16},{32,44},... | collective-permute-start | bytes 1572872 | tf_op jit(solution)/shard_map/ppermute | solution.py:22
  152.2 15.3 %collective-permute-start.53 = (bf16[304,1024]{1,0:T(8,128)(2,1)S(1)}, bf16[304,1024]{1,0:T(8,128)(2,1)S(1)}, u32[]{:S(2)}, u32[]{:S(2)}) collective-permute-start(bf16[304,1024]{1,0:T(8,128)(2,1)S(1)} %add_convert_fusion.7), channel_id=1, source_target_pairs={{0,2},{1,3},{2,0},{3,1},{4,6},{5,7},{6,4},{7,5},{8,10},{9,11},{10,... | collective-permute-start | bytes 1867784 | tf_op jit(solution)/shard_map/ppermute | solution.py:22
  181.3 15.5 %collective-permute-start.62 = (bf16[304,1024]{1,0:T(8,128)(2,1)S(1)}, bf16[304,1024]{1,0:T(8,128)(2,1)S(1)}, u32[]{:S(2)}, u32[]{:S(2)}) collective-permute-start(bf16[304,1024]{1,0:T(8,128)(2,1)S(1)} %add_convert_fusion.5.chip), channel_id=1, source_target_pairs={{0,2},{1,3},{2,0},{3,1},{4,6},{5,7},{6,4},{7,5},{8,10},{9,11},{10,... | collective-permute-start | bytes 1867784 | tf_op jit(solution)/shard_map/ppermute | solution.py:22
  213.7 15.6 %collective-permute-start.69 = (bf16[304,1024]{1,0:T(8,128)(2,1)S(1)}, bf16[304,1024]{1,0:T(8,128)(2,1)S(1)}, u32[]{:S(2)}, u32[]{:S(2)}) collective-permute-start(bf16[304,1024]{1,0:T(8,128)(2,1)S(1)} %add_convert_fusion.3.chip), channel_id=1, source_target_pairs={{0,2},{1,3},{2,0},{3,1},{4,6},{5,7},{6,4},{7,5},{8,10},{9,11},{10,... | collective-permute-start | bytes 1867784 | tf_op jit(solution)/shard_map/ppermute | solution.py:22
  238.6 15.7 %collective-permute-start.72 = (bf16[304,1024]{1,0:T(8,128)(2,1)S(1)}, bf16[304,1024]{1,0:T(8,128)(2,1)S(1)}, u32[]{:S(2)}, u32[]{:S(2)}) collective-permute-start(bf16[304,1024]{1,0:T(8,128)(2,1)S(1)} %add_convert_fusion.2.chip), channel_id=1, source_target_pairs={{0,2},{1,3},{2,0},{3,1},{4,6},{5,7},{6,4},{7,5},{8,10},{9,11},{10,... | collective-permute-start | bytes 1867784 | tf_op jit(solution)/shard_map/ppermute | solution.py:22
  239.5 14.0 %collective-permute-start.75 = (bf16[4,64,1024]{2,1,0:T(8,128)(2,1)S(1)}, bf16[4,64,1024]{2,1,0:T(8,128)(2,1)S(1)}, u32[]{:S(2)}, u32[]{:S(2)}) collective-permute-start(bf16[4,64,1024]{2,1,0:T(8,128)(2,1)S(1)} %get-tuple-element.365), channel_id=1, source_target_pairs={{0,12},{4,8},{8,4},{12,0},{16,28},{20,24},{24,20},{28,16},{32,44},... | collective-permute-start | bytes 1572872 | tf_op jit(solution)/shard_map/ppermute | solution.py:22
  240.6 13.7 %collective-permute-start.73 = (bf16[256,1024]{1,0:T(8,128)(2,1)S(1)}, bf16[256,1024]{1,0:T(8,128)(2,1)S(1)}, u32[]{:S(2)}, u32[]{:S(2)}) collective-permute-start(bf16[256,1024]{1,0:T(8,128)(2,1)S(1)} %get-tuple-element.360), channel_id=1, source_target_pairs={{0,48},{4,52},{8,56},{12,60},{16,32},{20,36},{24,40},{28,44},{32,1... | collective-permute-start | bytes 1572872 | tf_op jit(solution)/shard_map/ppermute | solution.py:22
  257.4 14.4 %collective-permute-start.78 = (bf16[128,1536]{1,0:T(8,128)(2,1)S(1)}, bf16[128,1536]{1,0:T(8,128)(2,1)S(1)}, u32[]{:S(2)}, u32[]{:S(2)}) collective-permute-start(bf16[128,1536]{1,0:T(8,128)(2,1)S(1)} %get-tuple-element.383), channel_id=1, source_target_pairs={{0,16},{4,20},{8,24},{12,28},{16,0},{20,4},{24,8},{28,12},{32,48},... | collective-permute-start | bytes 1179656 | tf_op jit(solution)/shard_map/ppermute | solution.py:22
  257.5 14.4 %collective-permute-start.79 = (bf16[128,1536]{1,0:T(8,128)(2,1)S(1)}, bf16[128,1536]{1,0:T(8,128)(2,1)S(1)}, u32[]{:S(2)}, u32[]{:S(2)}) collective-permute-start(bf16[128,1536]{1,0:T(8,128)(2,1)S(1)} %get-tuple-element.384), channel_id=1, source_target_pairs={{0,48},{4,52},{8,56},{12,60},{16,32},{20,36},{24,40},{28,44},{32,1... | collective-permute-start | bytes 1179656 | tf_op jit(solution)/shard_map/ppermute | solution.py:22
  258.8 13.1 %collective-permute-start.80 = (bf16[2,64,1536]{2,1,0:T(8,128)(2,1)S(1)}, bf16[2,64,1536]{2,1,0:T(8,128)(2,1)S(1)}, u32[]{:S(2)}, u32[]{:S(2)}) collective-permute-start(bf16[2,64,1536]{2,1,0:T(8,128)(2,1)S(1)} %get-tuple-element.388), channel_id=1, source_target_pairs={{0,4},{4,0},{8,12},{12,8},{16,20},{20,16},{24,28},{28,24},{32,36},... | collective-permute-start | bytes 1179656 | tf_op jit(solution)/shard_map/ppermute | solution.py:22
  286.1 25.5 %collective-permute-start.91 = (bf16[272,2048]{1,0:T(8,128)(2,1)S(1)}, bf16[272,2048]{1,0:T(8,128)(2,1)S(1)}, u32[]{:S(2)}, u32[]{:S(2)}) collective-permute-start(bf16[272,2048]{1,0:T(8,128)(2,1)S(1)} %get-tuple-element.433), channel_id=1, source_target_pairs={{0,48},{4,52},{8,56},{12,60},{16,32},{20,36},{24,40},{28,44},{32,1... | collective-permute-start | bytes 3342344 | tf_op jit(solution)/shard_map/ppermute | solution.py:22
  287.4 22.6 %collective-permute-start.92 = (bf16[256,2048]{1,0:T(8,128)(2,1)S(1)}, bf16[256,2048]{1,0:T(8,128)(2,1)S(1)}, u32[]{:S(2)}, u32[]{:S(2)}) collective-permute-start(bf16[256,2048]{1,0:T(8,128)(2,1)S(1)} %get-tuple-element.434), channel_id=1, source_target_pairs={{0,16},{4,20},{8,24},{12,28},{16,0},{20,4},{24,8},{28,12},{32,48},... | collective-permute-start | bytes 3145736 | tf_op jit(solution)/shard_map/ppermute | solution.py:22
  287.8 26.6 %collective-permute-start.87 = (bf16[4,64,2048]{2,1,0:T(8,128)(2,1)S(1)}, bf16[4,64,2048]{2,1,0:T(8,128)(2,1)S(1)}, u32[]{:S(2)}, u32[]{:S(2)}) collective-permute-start(bf16[4,64,2048]{2,1,0:T(8,128)(2,1)S(1)} %get-tuple-element.444), channel_id=1, source_target_pairs={{0,12},{4,8},{8,4},{12,0},{16,28},{20,24},{24,20},{28,16},{32,44},... | collective-permute-start | bytes 3145736 | tf_op jit(solution)/shard_map/ppermute | solution.py:22
  289.4 25.0 %collective-permute-start.88 = (bf16[4,64,2048]{2,1,0:T(8,128)(2,1)S(1)}, bf16[4,64,2048]{2,1,0:T(8,128)(2,1)S(1)}, u32[]{:S(2)}, u32[]{:S(2)}) collective-permute-start(bf16[4,64,2048]{2,1,0:T(8,128)(2,1)S(1)} %get-tuple-element.445), channel_id=1, source_target_pairs={{0,4},{4,0},{8,12},{12,8},{16,20},{20,16},{24,28},{28,24},{32,36},... | collective-permute-start | bytes 3145736 | tf_op jit(solution)/shard_map/ppermute | solution.py:22
  324.1 16.1 %collective-permute-start.101 = (bf16[80,3072]{1,0:T(8,128)(2,1)S(1)}, bf16[80,3072]{1,0:T(8,128)(2,1)S(1)}, u32[]{:S(2)}, u32[]{:S(2)}) collective-permute-start(bf16[80,3072]{1,0:T(8,128)(2,1)S(1)} %get-tuple-element.484), channel_id=1, source_target_pairs={{0,12},{4,8},{8,4},{12,0},{16,28},{20,24},{24,20},{28,16},{32,44},... | collective-permute-start | bytes 1474568 | tf_op jit(solution)/shard_map/ppermute | solution.py:22
  325.5 14.7 %collective-permute-start.102 = (bf16[64,3072]{1,0:T(8,128)(2,1)S(1)}, bf16[64,3072]{1,0:T(8,128)(2,1)S(1)}, u32[]{:S(2)}, u32[]{:S(2)}) collective-permute-start(bf16[64,3072]{1,0:T(8,128)(2,1)S(1)} %get-tuple-element.486), channel_id=1, source_target_pairs={{0,4},{4,0},{8,12},{12,8},{16,20},{20,16},{24,28},{28,24},{32,36},... | collective-permute-start | bytes 1179656 | tf_op jit(solution)/shard_map/ppermute | solution.py:22
  (85 other events, 692.7 us)
